TPU v7x, 32 devices: a whole 2x2x4 slice. The times are simulated.
32 devices in a mesh: parts: 1, dp: 2 (over core), group: 16 (over z, y, x).
Axes of the slice: x: 2, y: 2, z: 4, core: 2. Of those that a mesh axis runs over, the one named last changes fastest.
Arguments:
- hidden_in: bfloat16 [4, 256, 2048], P(('parts', 'dp'), 'group'), may hold values from -6 to 6
- span_lengths: int32 [4], P('parts'), may hold values from 0 to 256, as said below
- norm_gain: bfloat16 [2048], replicated, may hold values from 0.099609375 to 1.8984375
- query_weight: bfloat16 [2048, 2048], P(None, 'group'), may hold values from -8 to 8
- key_weight: bfloat16 [2048, 256], P(None, 'group'), may hold values from -0.5 to 0.5
- value_weight: bfloat16 [2048, 256], P(None, 'group'), may hold values from -0.125 to 0.125
- out_weight: bfloat16 [2048, 2048], P('group'), may hold values from -0.5 to 0.5
Outputs:
- hidden_out: bfloat16 [4, 256, 2048], P(('parts', 'dp'), 'group')
Inputs may be any that keep to these rules, and one draw needn't show every extreme that they name: `span_lengths`: live spans (length above 0) are the leading slots of a dp index; in each part one dp index holds 2 live spans and the other none; the first live span is full.
All inputs are finite; a program needn't handle non-finite values.
Results may differ from a plain program's by a relative error of at most 0.0068.
Values may be sent and summed in bfloat16 or wider, within the bound.
A program may use at most 64 MiB of HBM per device.

v0:
```python
import math

import jax
import jax.numpy as jnp
from jax import lax
from jax.sharding import PartitionSpec as P


def partner_2(block, axis, stride):
    count = lax.axis_size(axis)
    route = []
    for low in range(count):
        high = low | 1 << stride
        if high != low and high < count:
            route += [(low, high), (high, low)]
    return lax.ppermute(block, axis, route)


def rms_rows(rows, gain):
    wide = rows.astype(jnp.float32)
    scale = lax.rsqrt(jnp.mean(wide * wide, axis=-1, keepdims=True) + 1e-05)
    return (wide * scale * gain.astype(jnp.float32)).astype(jnp.bfloat16)


def rotate(block):
    count = block.shape[-2]
    width = block.shape[-1]
    half = width // 2
    positions = jnp.arange(count, dtype=jnp.float32)
    freqs = jnp.exp(-math.log(500000.0) * 2.0 * jnp.arange(half, dtype=jnp.float32) / width)
    angles = positions[:, None] * freqs[None, :]
    cosine = jnp.cos(angles)
    sine = jnp.sin(angles)
    first = block[..., :half]
    second = block[..., half:]
    return jnp.concatenate(
        [first * cosine - second * sine, second * cosine + first * sine], axis=-1
    )


def attend(span_rows, lengths, norm_gain, query_weight, key_weight, value_weight, out_weight):
    count, rows, width = span_rows.shape
    groups = lax.axis_size("group")
    span = rows * groups
    head_size = query_weight.shape[1]
    key_cols = key_weight.shape[1]
    normed = rms_rows(span_rows, norm_gain)
    joined = jnp.concatenate([query_weight, key_weight, value_weight], axis=1)
    projected = jnp.einsum(
        "prd,dc->prc",
        lax.all_gather(normed, "group", axis=1, tiled=True),
        joined,
        preferred_element_type=jnp.float32,
    ).astype(jnp.bfloat16)
    query = rotate(projected[..., :head_size].astype(jnp.float32)).astype(jnp.bfloat16)
    key_stack = jnp.swapaxes(projected[..., head_size : head_size + key_cols], 1, 2)
    value_stack = jnp.swapaxes(projected[..., head_size + key_cols :], 1, 2)
    my_index = lax.axis_index("group")
    levels = (head_size // key_cols).bit_length() - 1
    for level in range(levels):
        partner = partner_2((key_stack, value_stack), "group", level)
        first_half = my_index // (1 << level) % 2 == 0
        key_stack = jnp.where(
            first_half,
            jnp.concatenate([key_stack, partner[0]], axis=1),
            jnp.concatenate([partner[0], key_stack], axis=1),
        )
        value_stack = jnp.where(
            first_half,
            jnp.concatenate([value_stack, partner[1]], axis=1),
            jnp.concatenate([partner[1], value_stack], axis=1),
        )
    keys = rotate(jnp.swapaxes(key_stack, 1, 2).astype(jnp.float32)).astype(jnp.bfloat16)
    scores = jnp.einsum(
        "pqd,pkd->pqk", query, keys, preferred_element_type=jnp.float32
    ) / math.sqrt(head_size)
    qpos = jnp.arange(span, dtype=jnp.int32)[None, :, None]
    kpos = jnp.arange(span, dtype=jnp.int32)[None, None, :]
    allowed = kpos <= qpos
    scores = jnp.where(allowed, scores, -1e30)
    peak = jnp.max(scores, axis=-1, keepdims=True)
    expo = jnp.exp(scores - peak)
    weights = (expo / jnp.sum(expo, axis=-1, keepdims=True)).astype(jnp.bfloat16)
    heads_out = jnp.einsum(
        "pqk,pdk->pqd", weights, value_stack, preferred_element_type=jnp.float32
    ).astype(jnp.bfloat16)
    head_rows = jnp.swapaxes(heads_out, 0, 1).reshape(span * count, head_size)
    mixed = lax.psum_scatter(
        jnp.dot(head_rows, out_weight, preferred_element_type=jnp.float32),
        "group",
        scatter_dimension=0,
        tiled=True,
    )
    mixed = jnp.swapaxes(mixed.reshape(rows, count, width), 0, 1)
    row_ids = my_index * rows + jnp.arange(rows, dtype=jnp.int32)
    live = row_ids[None, :] < lengths[:, None]
    return jnp.where(live[..., None], span_rows.astype(jnp.float32) + mixed, 0.0).astype(
        jnp.bfloat16
    )


def shards(hidden_in, span_lengths, norm_gain, query_weight, key_weight, value_weight, out_weight):
    slots = hidden_in.shape[0]
    dp_index = lax.axis_index("dp")
    own_lengths = lax.dynamic_slice_in_dim(span_lengths, dp_index * slots, slots)
    return attend(
        hidden_in, own_lengths, norm_gain, query_weight, key_weight, value_weight, out_weight
    )


def solution(mesh):
    placed = (
        P(("parts", "dp"), "group", None),
        P("parts"),
        P(),
        P(None, "group"),
        P(None, "group"),
        P(None, "group"),
        P("group", None),
    )
    return jax.shard_map(
        shards,
        mesh=mesh,
        in_specs=placed,
        out_specs=P(("parts", "dp"), "group", None),
        check_vma=False,
    )
```

profile of v0, /device:TPU:0, one launch (start us, length us, event | category | flops | bytes accessed | tf_op | source)
XLA Modules:
  0.0 195.5 jit_solution(15160337258598796745)
XLA Ops:
  6.5 1.1 fusion.9
  7.6 0.7 convert_element_type.38
  8.3 1.7 fusion.11
  10.1 1.2 copy.12
  11.4 0.3 fusion.27
  11.7 61.8 %all-gather.2.cloned.1.call-done = bf16[2,256,2048]{2,1,0:T(8,128)(2,1)} async-done(((bf16[2,16,2048]{2,1,0:T(8,128)(2,1)}), bf16[2,256,2048]{2,1,0:T(8,128)(2,1)}) %all-gather.2.cloned.1.call-update) | async-done | bytes 2097168 | tf_op jit(solution)/shard_map/all_gather | solution.py:51
  73.5 2.4 %convolution_convert_fusion = bf16[2,256,160]{1,2,0:T(8,128)(2,1)S(1)} fusion(bf16[2,256,2048]{2,1,0:T(8,128)(2,1)} %all-gather.2.cloned.1.call-done, bf16[2048,16]{0,1:T(8,128)(2,1)} %param.12, bf16[2048,16]{0,1:T(8,128)(2,1)} %param.11, bf16[2048,128]{0,1:T(8,128)(2,1)S(1)} %copy.12), kind=kOutput, calls=%fused_computation.5 | convolution fusion | flops 337592320 | bytes 2916352 | tf_op jit(solution)/shard_map/prd,dc->prc/dot_general | solution.py:49
  76.0 1.5 collective-permute-start
  77.5 0.6 collective-permute-start.3
  78.2 1.6 collective-permute-done
  79.8 1.5 collective-permute-start.1
  81.4 0.6 collective-permute-start.4
  82.0 1.8 collective-permute-done.1
  83.8 1.6 collective-permute-start.2
  85.4 1.5 collective-permute-start.5
  87.0 1.2 collective-permute-done.2
  88.5 0.4 fusion.40
  88.9 0.9 collective-permute-done.5
  89.8 0.4 fusion.4
  90.3 2.6 %fusion.45 = f32[512,2048]{1,0:T(8,128)} fusion(bf16[512,128]{1,0:T(8,128)(2,1)S(1)} %bitcast.18, bf16[128,2048]{1,0:T(8,128)(2,1)S(1)} %copy-done), kind=kOutput, calls=%fused_computation.64 | convolution fusion | flops 268435456 | bytes 4849664 | tf_op jit(solution)/shard_map/dot_general | solution.py:89
  92.9 0.6 copy-done.2
  93.7 93.0 %reduce-scatter.2.cloned.1.call-done = f32[32,2048]{1,0:T(8,128)} async-done(((f32[512,2048]{1,0:T(8,128)}), f32[32,2048]{1,0:T(8,128)}) %reduce-scatter.2.cloned.1.call-update) | async-done | bytes 262160 | tf_op jit(solution)/shard_map/reduce_scatter | solution.py:88
  186.7 1.1 reshape.110
  187.8 0.8 fusion.13
  (27 shorter events, 0.9 us)
Async XLA Ops:
  6.5 83.7 %copy-start = (bf16[128,2048]{1,0:T(8,128)(2,1)S(1)}, bf16[128,2048]{1,0:T(8,128)(2,1)}, u32[]{:S(2)}) copy-start(bf16[128,2048]{1,0:T(8,128)(2,1)} %param.13) | copy-start | bytes 1572868
  6.5 67.0 %all-gather.2.cloned.1.call-start = ((), (), s32[]{:S(2)}) async-start(), calls=%async_computation.1 | async-start | bytes 2228224 | tf_op jit(solution)/shard_map/all_gather | solution.py:51
  10.0 176.7 %reduce-scatter.2.cloned.1.call-start = ((), (), s32[]{:S(2)}) async-start(), calls=%async_computation.2 | async-start | bytes 4456448 | tf_op jit(solution)/shard_map/reduce_scatter | solution.py:88
  76.0 3.8 %collective-permute-start = (bf16[2,16,256]{2,1,0:T(8,128)(2,1)S(1)}, bf16[2,16,256]{2,1,0:T(8,128)(2,1)S(1)}, u32[]{:S(2)}, u32[]{:S(2)}) collective-permute-start(bf16[2,16,256]{2,1,0:T(8,128)(2,1)S(1)} %get-tuple-element.10), channel_id=1, source_target_pairs={{0,1},{1,0},{2,3},{3,2},{4,5},{5,4},{6,7},{7,6},{8,9},{9,8},{10,11... | collective-permute-start | bytes 49160 | tf_op jit(solution)/shard_map/ppermute | solution.py:16
  77.5 3.8 %collective-permute-start.3 = (bf16[2,16,256]{2,1,0:T(8,128)(2,1)S(1)}, bf16[2,16,256]{2,1,0:T(8,128)(2,1)S(1)}, u32[]{:S(2)}, u32[]{:S(2)}) collective-permute-start(bf16[2,16,256]{2,1,0:T(8,128)(2,1)S(1)} %get-tuple-element.9), channel_id=1, source_target_pairs={{0,1},{1,0},{2,3},{3,2},{4,5},{5,4},{6,7},{7,6},{8,9},{9,8},{10,11... | collective-permute-start | bytes 49160 | tf_op jit(solution)/shard_map/ppermute | solution.py:16
  79.8 4.0 %collective-permute-start.1 = (bf16[2,32,256]{2,1,0:T(8,128)(2,1)S(1)}, bf16[2,32,256]{2,1,0:T(8,128)(2,1)S(1)}, u32[]{:S(2)}, u32[]{:S(2)}) collective-permute-start(bf16[2,32,256]{2,1,0:T(8,128)(2,1)S(1)} %maximum_select_fusion.5), channel_id=1, source_target_pairs={{0,2},{2,0},{1,3},{3,1},{4,6},{6,4},{5,7},{7,5},{8,10},{10,8},{9,1... | collective-permute-start | bytes 98312 | tf_op jit(solution)/shard_map/ppermute | solution.py:16
  81.4 4.1 %collective-permute-start.4 = (bf16[2,32,256]{2,1,0:T(8,128)(2,1)S(1)}, bf16[2,32,256]{2,1,0:T(8,128)(2,1)S(1)}, u32[]{:S(2)}, u32[]{:S(2)}) collective-permute-start(bf16[2,32,256]{2,1,0:T(8,128)(2,1)S(1)} %maximum_select_fusion.6), channel_id=1, source_target_pairs={{0,2},{2,0},{1,3},{3,1},{4,6},{6,4},{5,7},{7,5},{8,10},{10,8},{9,1... | collective-permute-start | bytes 98312 | tf_op jit(solution)/shard_map/ppermute | solution.py:16
  83.8 4.3 %collective-permute-start.2 = (bf16[2,64,256]{2,1,0:T(8,128)(2,1)S(1)}, bf16[2,64,256]{2,1,0:T(8,128)(2,1)S(1)}, u32[]{:S(2)}, u32[]{:S(2)}) collective-permute-start(bf16[2,64,256]{2,1,0:T(8,128)(2,1)S(1)} %maximum_select_fusion.3), channel_id=1, source_target_pairs={{0,4},{4,0},{1,5},{5,1},{2,6},{6,2},{3,7},{7,3},{8,12},{12,8},{9,1... | collective-permute-start | bytes 196616 | tf_op jit(solution)/shard_map/ppermute | solution.py:16
  85.4 4.3 %collective-permute-start.5 = (bf16[2,64,256]{2,1,0:T(8,128)(2,1)S(1)}, bf16[2,64,256]{2,1,0:T(8,128)(2,1)S(1)}, u32[]{:S(2)}, u32[]{:S(2)}) collective-permute-start(bf16[2,64,256]{2,1,0:T(8,128)(2,1)S(1)} %maximum_select_fusion.4), channel_id=1, source_target_pairs={{0,4},{4,0},{1,5},{5,1},{2,6},{6,2},{3,7},{7,3},{8,12},{12,8},{9,1... | collective-permute-start | bytes 196616 | tf_op jit(solution)/shard_map/ppermute | solution.py:16
  92.9 0.7 copy-start.2
  92.9 94.9 %copy-start.1 = (bf16[2,16,2048]{2,1,0:T(8,128)(2,1)S(1)}, bf16[2,16,2048]{2,1,0:T(8,128)(2,1)}, u32[]{:S(2)}) copy-start(bf16[2,16,2048]{2,1,0:T(8,128)(2,1)} %param.7) | copy-start | bytes 393220
Sparse Core Ops, SparseCore 0:
  10.1 63.3 all-gather.1
  93.1 93.6 reduce-scatter.1
where the time goes:
time: 196 us; the launch traced here: 195 us
  waiting for transfers between devices  160 us (82%)
  between operations  13.6 us (7%)
  starting transfers between devices  7.5 us (4%)
  matrix products  6.09 us (3%)
  other arithmetic  4.84 us (2%)
  local copies, waits for them, and re-layouts  3.19 us (2%)
    reduce_scatter x1, waiting for transfers between devices, attend(): lax.psum_scatter(jnp.dot(head_rows, out_weight, preferred_element_type=jn...  93 us
    all_gather x1, waiting for transfers between devices, attend(): lax.all_gather(normed, 'group', axis=1, tiled=True)  61.8 us
    ppermute x6, starting transfers between devices, partner_2(): return lax.ppermute(block, axis, route)  7.45 us
    ppermute x6, waiting for transfers between devices, partner_2(): return lax.ppermute(block, axis, route)  5.46 us
  transfers between devices with their start and end apart: 8, of which 6 were waited for; matrix products, arithmetic and copies ran while one was open for 1% of the time, Pallas kernels for 0%

commit v1 on v0

--- a/solution.py
+++ b/solution.py
@@ -2,8 +2,13 @@
 
 import jax
 import jax.numpy as jnp
+import numpy as np
 from jax import lax
+from jax.experimental import pallas as pl
+from jax.experimental.pallas import tpu as pltpu
 from jax.sharding import PartitionSpec as P
+
+MESH = pl.DeviceIdType.MESH
 
 
 def partner_2(block, axis, stride):
@@ -99,8 +104,279 @@
     )
 
 
+def slot_positions(count):
+    at = np.arange(count)
+    return (at // 16 % 4) * 64 + (at // 64) * 16 + at % 16
+
+
+def tables(span, width):
+    half = width // 2
+    freqs = 500000.0 ** (-2.0 * np.arange(half) / width)
+    angles = slot_positions(span)[:, None] * freqs[None, :]
+    cosine, sine = np.cos(angles), np.sin(angles)
+    wide_cos = np.concatenate([cosine, cosine], axis=1).astype(np.float32)
+    wide_sin = np.concatenate([-sine, sine], axis=1).astype(np.float32)
+    return wide_cos, wide_sin, cosine.T.astype(np.float32), sine.T.astype(np.float32)
+
+
+SWAP, GZ, GX, GY, GD, KV, RD, RX, RY, RZ, BACK, COUNT = 0, 1, 5, 9, 13, 17, 33, 37, 41, 45, 49, 50
+
+
+def span_kernel(
+    lens, hidden, gain, wq, wk, wv, wo, cosq, sinq, cosk, sink, out,
+    swap_buf, own_rows, x, wqv, wkn, wvn, wov, q, kv, heads, part, out_send, rd, rx, ry, rz, fin, fin_in,
+    send, recv, local,
+):
+    d = lax.axis_index("dp")
+    g = lax.axis_index("group")
+    z, c = g // 4, g % 4
+    zs = (z, z + 1 - 2 * (z % 2), (z + 2) % 4, 3 - z)
+    cs = (c, c + 1 - 2 * (c % 2), (c + 2) % 4, 3 - c)
+
+    def chip(zk, ck):
+        return {"group": zs[zk] * 4 + cs[ck]}
+
+    near_x, near_y = chip(0, 1), chip(0, 2)
+    sibling = {"dp": 1 - d}
+    kv_peers = [(k // 4, k % 4) for k in range(1, 8)]
+    greeted = [sibling] + [chip(*peer) for peer in kv_peers] + [chip(2, 0), chip(3, 0)]
+
+    loads = [
+        pltpu.make_async_copy(wk, wkn, local.at[0]),
+        pltpu.make_async_copy(wv, wvn, local.at[1]),
+        pltpu.make_async_copy(wq, wqv, local.at[2]),
+        pltpu.make_async_copy(wo, wov, local.at[3]),
+    ]
+    for load in loads:
+        load.start()
+
+    barrier = pltpu.get_barrier_semaphore()
+    for device in greeted:
+        pl.semaphore_signal(barrier, inc=1, device_id=device, device_id_type=MESH)
+    pl.semaphore_wait(barrier, len(greeted))
+
+    started = []
+
+    def push(source, target, sent, received, device):
+        copy = pltpu.make_async_remote_copy(
+            src_ref=source, dst_ref=target, send_sem=send.at[sent], recv_sem=recv.at[received],
+            device_id=device, device_id_type=MESH,
+        )
+        copy.start()
+        started.append(copy)
+
+    def take(target, received):
+        pltpu.make_async_remote_copy(
+            src_ref=target, dst_ref=target, send_sem=send.at[received], recv_sem=recv.at[received],
+            device_id=sibling, device_id_type=MESH,
+        ).wait_recv()
+
+    push(hidden.at[1 - d], swap_buf, SWAP, SWAP, sibling)
+    busy = jnp.where(lens[0] > 0, 0, 1)
+    length = jnp.where(busy == 0, lens[d], lens[2 + d])
+    take(swap_buf, SWAP)
+    rows = jnp.where(busy == d, hidden[d].astype(jnp.float32), swap_buf[...].astype(jnp.float32))
+    own_rows[...] = rows
+    scale = lax.rsqrt(jnp.mean(rows * rows, axis=-1, keepdims=True) + 1e-05)
+
+    def slot(ck, zk):
+        return cs[ck] * 4 + zs[zk]
+
+    def block(ck, zk):
+        return x.at[slot(ck, zk)]
+
+    x[slot(0, 0)] = (rows * scale * gain[...].astype(jnp.float32)).astype(jnp.bfloat16)
+
+    def spread(k):
+        push(block(0, k), block(0, k), GX + k, GX + k, near_x)
+        push(block(0, k), block(0, k), GY + k, GY + k, near_y)
+
+    for k in (1, 2, 3):
+        push(block(0, 0), block(0, 0), GZ + k, GZ + k, chip(k, 0))
+    spread(0)
+
+    def relay(k):
+        if k % 2 == 0:
+            take(block(1, k), GX + k)
+            push(block(1, k), block(1, k), GD + k, GD + k, near_y)
+        else:
+            take(block(2, k), GY + k)
+            push(block(2, k), block(2, k), GD + k, GD + k, near_x)
+
+    take(block(0, 1), GZ + 1)
+    spread(1)
+    relay(0)
+    take(block(0, 2), GZ + 2)
+    spread(2)
+    relay(1)
+    take(block(0, 3), GZ + 3)
+    spread(3)
+    relay(2)
+    relay(3)
+
+    for load in loads:
+        load.wait()
+
+    member = g % 8
+
+    def project(half):
+        lines = x[pl.ds(half * 8, 8)].reshape(128, x.shape[2])
+        q[pl.ds(half * 128, 128), :] = jnp.dot(lines, wqv[...], preferred_element_type=jnp.float32).astype(jnp.bfloat16)
+        keys = jnp.dot(lines, wkn[...], preferred_element_type=jnp.float32)
+        values = jnp.dot(lines, wvn[...], preferred_element_type=jnp.float32)
+        kv[half, member, 0:16, :] = keys.T.astype(jnp.bfloat16)
+        kv[half, member, 16:32, :] = values.T.astype(jnp.bfloat16)
+        for k, peer in enumerate(kv_peers, 1):
+            index = KV + half * 8 + k
+            push(kv.at[half, member], kv.at[half, member], index, index, chip(*peer))
+
+    first = c // 2
+    take(block(1, 1), GX + 1)
+    take(block(1, 3), GX + 3)
+    project(first)
+    take(block(2, 0), GY)
+    take(block(2, 2), GY + 2)
+    for k in range(4):
+        take(block(3, k), GD + k)
+    project(1 - first)
+
+    wide = q[...].astype(jnp.float32)
+    query = (wide * cosq[...] + pltpu.roll(wide, 64, 1) * sinq[...]).astype(jnp.bfloat16)
+    for half in range(2):
+        for k, (zk, ck) in enumerate(kv_peers, 1):
+            take(kv.at[half, (zs[zk] % 2) * 4 + cs[ck]], KV + half * 8 + k)
+
+    def joined(low):
+        return jnp.concatenate([kv[half, :, low : low + 16, :].reshape(128, 128) for half in range(2)], axis=1)
+
+    keys = joined(0).astype(jnp.float32)
+    upper, lower = keys[:64], keys[64:]
+    turned = jnp.concatenate(
+        [upper * cosk[...] - lower * sink[...], lower * cosk[...] + upper * sink[...]], axis=0
+    ).astype(jnp.bfloat16)
+    scores = jnp.dot(query, turned, preferred_element_type=jnp.float32) * (1.0 / math.sqrt(128))
+
+    def position(dim):
+        at = lax.broadcasted_iota(jnp.int32, scores.shape, dim)
+        return ((at >> 4) & 3) * 64 + (at >> 6) * 16 + (at & 15)
+
+    scores = jnp.where(position(1) <= position(0), scores, -1e30)
+    expo = jnp.exp(scores - jnp.max(scores, axis=-1, keepdims=True))
+    weights = (expo / jnp.sum(expo, axis=-1, keepdims=True)).astype(jnp.bfloat16)
+    heads[...] = lax.dot_general(
+        weights, joined(16), (((1,), (1,)), ((), ())), preferred_element_type=jnp.float32
+    ).astype(jnp.bfloat16)
+
+    def partial(ck):
+        mine = heads[pl.ds(cs[ck] * 64, 64), :]
+        return jnp.dot(mine, wov[...], preferred_element_type=jnp.float32).reshape(4, 16, wov.shape[1])
+
+    out_send[pl.ds(cs[3] * 4, 4)] = partial(3).astype(jnp.bfloat16)
+    for k in (2, 3, 0, 1):
+        push(out_send.at[slot(3, k)], rd.at[k], RD + k, RD + k, near_x if k % 2 == 0 else near_y)
+    part[pl.ds(cs[1] * 4, 4)] = partial(1)
+    part[pl.ds(cs[2] * 4, 4)] = partial(2)
+
+    def hand_on(ck, k, with_relayed):
+        own = part[slot(ck, k)]
+        if with_relayed:
+            take(rd.at[k], RD + k)
+            own = own + rd[k].astype(jnp.float32)
+        out_send[slot(ck, k)] = own.astype(jnp.bfloat16)
+        if ck == 1:
+            push(out_send.at[slot(1, k)], rx.at[k], RX + k, RX + k, near_x)
+        else:
+            push(out_send.at[slot(2, k)], ry.at[k], RY + k, RY + k, near_y)
+
+    for k in (2, 3, 0, 1):
+        hand_on(1 if k % 2 == 0 else 2, k, False)
+    part[pl.ds(cs[0] * 4, 4)] = partial(0)
+    for k in (2, 3, 0, 1):
+        hand_on(2 if k % 2 == 0 else 1, k, True)
+
+    def column_sum(k):
+        take(rx.at[k], RX + k)
+        take(ry.at[k], RY + k)
+        return part[slot(0, k)] + rx[k].astype(jnp.float32) + ry[k].astype(jnp.float32)
+
+    for k in (2, 3, 1):
+        out_send[slot(0, k)] = column_sum(k).astype(jnp.bfloat16)
+        push(out_send.at[slot(0, k)], rz.at[k], RZ + k, RZ + k, chip(k, 0))
+    total = column_sum(0)
+    for k in (2, 3, 1):
+        take(rz.at[k], RZ + k)
+        total = total + rz[k].astype(jnp.float32)
+    ids = g * 16 + lax.broadcasted_iota(jnp.int32, total.shape, 0)
+    fin[...] = jnp.where(ids < length, own_rows[...] + total, 0.0).astype(jnp.bfloat16)
+    push(fin, fin_in, BACK, BACK, sibling)
+    out[d] = fin[...]
+    take(fin_in, BACK)
+    out[1 - d] = fin_in[...]
+    for copy in started:
+        copy.wait_send()
+
+
+def fused(hidden_in, span_lengths, norm_gain, query_weight, key_weight, value_weight, out_weight):
+    slots, rows, width = hidden_in.shape
+    head_size = query_weight.shape[1]
+    span = rows * 16
+    vmem = pl.BlockSpec(memory_space=pltpu.VMEM)
+    anywhere = pl.BlockSpec(memory_space=pl.ANY)
+    bf16, f32 = jnp.bfloat16, jnp.float32
+    result = pl.pallas_call(
+        span_kernel,
+        out_shape=jax.ShapeDtypeStruct(hidden_in.shape, bf16),
+        in_specs=[pl.BlockSpec(memory_space=pltpu.SMEM), vmem, vmem] + [anywhere] * 4 + [vmem] * 4,
+        out_specs=vmem,
+        scratch_shapes=[
+            pltpu.VMEM((rows, width), bf16),
+            pltpu.VMEM((rows, width), f32),
+            pltpu.VMEM((16, rows, width), bf16),
+            pltpu.VMEM(query_weight.shape, bf16),
+            pltpu.VMEM(key_weight.shape, bf16),
+            pltpu.VMEM(value_weight.shape, bf16),
+            pltpu.VMEM(out_weight.shape, bf16),
+            pltpu.VMEM((span, head_size), bf16),
+            pltpu.VMEM((2, 8, 32, 128), bf16),
+            pltpu.VMEM((span, head_size), bf16),
+            pltpu.VMEM((16, rows, width), f32),
+            pltpu.VMEM((16, rows, width), bf16),
+            pltpu.VMEM((4, rows, width), bf16),
+            pltpu.VMEM((4, rows, width), bf16),
+            pltpu.VMEM((4, rows, width), bf16),
+            pltpu.VMEM((4, rows, width), bf16),
+            pltpu.VMEM((rows, width), bf16),
+            pltpu.VMEM((rows, width), bf16),
+            pltpu.SemaphoreType.DMA((COUNT,)),
+            pltpu.SemaphoreType.DMA((COUNT,)),
+            pltpu.SemaphoreType.DMA((4,)),
+        ],
+        compiler_params=pltpu.CompilerParams(
+            collective_id=0, has_side_effects=True, vmem_limit_bytes=32 * 1024 * 1024
+        ),
+        cost_estimate=pl.CostEstimate(
+            flops=4 * span * width * head_size, bytes_accessed=4 * width * head_size, transcendentals=span * span
+        ),
+    )(
+        span_lengths, hidden_in, norm_gain.reshape(1, width), query_weight, key_weight, value_weight,
+        out_weight, *tables(span, head_size),
+    )
+    holds = lax.dynamic_index_in_dim(span_lengths, lax.axis_index("dp") * slots, keepdims=False) > 0
+    return jnp.where(holds, result, jnp.zeros_like(result))
+
+
 def shards(hidden_in, span_lengths, norm_gain, query_weight, key_weight, value_weight, out_weight):
     slots = hidden_in.shape[0]
+    if (
+        lax.axis_size("group") == 16
+        and lax.axis_size("dp") == 2
+        and hidden_in.shape[:2] == (2, 16)
+        and query_weight.shape[1] == 128
+        and key_weight.shape[1] == 16
+    ):
+        return fused(
+            hidden_in, span_lengths, norm_gain, query_weight, key_weight, value_weight, out_weight
+        )
     dp_index = lax.axis_index("dp")
     own_lengths = lax.dynamic_slice_in_dim(span_lengths, dp_index * slots, slots)
     return attend(

time: 196 us -> 52.1 us (0.27)
  waiting for transfers between devices: 160 us -> 0 us
  Pallas kernels: 0 us -> 43.2 us
  between operations: 13.6 us -> 0.74 us
  starting transfers between devices: 7.5 us -> 0 us
  matrix products: 6.09 us -> 0 us
  other arithmetic: 4.84 us -> 0.67 us
  local copies, waits for them, and re-layouts: 3.19 us -> 7.14 us
    reduce_scatter x1 -> x0, waiting for transfers between devices: 93 us -> none  [attend(): lax.psum_scatter(jnp.dot(head_rows, out_weight, preferred_element_type=jn...]
    all_gather x1 -> x0, waiting for transfers between devices: 61.8 us -> none  [attend(): lax.all_gather(normed, 'group', axis=1, tiled=True)]
    pallas_call x0 -> x1, Pallas kernels: none -> 43.2 us  [fused(): pl.pallas_call(span_kernel, out_shape=jax.ShapeDtypeStruct(hidden_in.shap...]
    ppermute x6 -> x0, starting transfers between devices: 7.45 us -> none  [partner_2(): return lax.ppermute(block, axis, route)]
    dot_general x4 -> x0, matrix products: 5.7 us -> none  [the longest x1 2.64 us: attend(): jnp.dot(head_rows, out_weight, preferred_element_type=jnp.float32)]
    ppermute x6 -> x0, waiting for transfers between devices: 5.46 us -> none  [partner_2(): return lax.ppermute(block, axis, route)]
    unnamed x7 -> x18, local copies, waits for them, and re-layouts: 1.88 us -> 5.84 us
    convert_element_type x5 -> x0, other arithmetic: 3.22 us -> none  [the longest x2 2.36 us: rms_rows(): return (wide * scale * gain.astype(jnp.float32)).astype(jnp.bfloat16)]
  transfers between devices with their start and end apart: 8 -> 0, of which waited for: 6 -> 0; matrix products, arithmetic and copies ran while one was open for 1% -> 0% of each run, Pallas kernels for 0% -> 0%
where the time goes in v1:
time: 52.1 us; the launch traced here: 51.7 us
  Pallas kernels  43.2 us (83%)
  local copies, waits for them, and re-layouts  7.14 us (14%)
  between operations  0.74 us (1%)
  other arithmetic  0.67 us (1%)
    pallas_call x1, Pallas kernels, fused(): pl.pallas_call(span_kernel, out_shape=jax.ShapeDtypeStruct(hidden_in.shap...  43.2 us
    unnamed x18, local copies, waits for them, and re-layouts  5.84 us

profile of v1, /device:TPU:0, one launch (start us, length us, event | category | flops | bytes accessed | tf_op | source)
XLA Modules:
  0.0 51.7 jit_solution(16851603963982555732)
XLA Ops:
  0.0 0.0 copy-start.7
  0.0 0.7 %reshape.5.gain = bf16[1,2048]{1,0:T(2,128)(2,1)S(1)} reshape(bf16[2048]{0:T(1024)(128)(2,1)} %param.13) | data formatting | bytes 8192 | tf_op jit(solution)/shard_map/reshape | solution.py:361
  0.7 0.0 copy-start
  0.7 0.0 copy-start.1
  0.7 1.2 %copy.12.wk = bf16[2048,16]{1,0:T(8,128)(2,1)S(1)} copy(bf16[2048,16]{0,1:T(8,128)(2,1)} %param.15) | data formatting | bytes 131072 | tf_op args[4]
  1.9 0.0 copy-start.2
  1.9 1.1 %copy.13.wv = bf16[2048,16]{1,0:T(8,128)(2,1)S(1)} copy(bf16[2048,16]{0,1:T(8,128)(2,1)} %param.16) | data formatting | bytes 131072 | tf_op args[5]
  3.1 0.0 copy-done.7
  3.1 0.0 copy-done
  3.1 0.0 copy-done.1
  3.1 0.0 copy-done.2
  3.1 0.0 copy-start.3
  3.1 0.9 %copy-done.3 = f32[256,128]{1,0:T(8,128)S(1)} copy-done((f32[256,128]{1,0:T(8,128)S(1)}, f32[256,128]{1,0:T(8,128)}, u32[]{:S(2)}) %copy-start.3) | copy-done | bytes 131096
  4.0 0.0 copy-start.4
  4.0 0.9 %copy-done.4 = f32[256,128]{1,0:T(8,128)S(1)} copy-done((f32[256,128]{1,0:T(8,128)S(1)}, f32[256,128]{1,0:T(8,128)}, u32[]{:S(2)}) %copy-start.4) | copy-done | bytes 131096
  4.9 0.0 copy-start.5
  4.9 0.8 %copy-done.5 = f32[64,256]{1,0:T(8,128)S(1)} copy-done((f32[64,256]{1,0:T(8,128)S(1)}, f32[64,256]{1,0:T(8,128)}, u32[]{:S(2)}) %copy-start.5) | copy-done | bytes 65560
  5.8 0.0 copy-start.6
  5.8 0.8 %copy-done.6 = f32[64,256]{1,0:T(8,128)S(1)} copy-done((f32[64,256]{1,0:T(8,128)S(1)}, f32[64,256]{1,0:T(8,128)}, u32[]{:S(2)}) %copy-start.6) | copy-done | bytes 65560
  6.6 43.2 %shard_map.109 = bf16[2,16,2048]{2,1,0:T(8,128)(2,1)S(1)} custom-call(s32[4]{0:T(128)S(1)} %copy-done.7, bf16[2,16,2048]{2,1,0:T(8,128)(2,1)S(1)} %copy-done.2, bf16[1,2048]{1,0:T(2,128)(2,1)S(1)} %reshape.5.gain, bf16[2048,128]{1,0:T(8,128)(2,1)S(1)} %copy-done, bf16[2048,16]{1,0:T(8,128)(2,1)S(1)} %copy.12.wk, bf16[2048,16]{1,0:T(8,128)(2,1)S(1)} %copy.13.wv, ...), custom_call_target="tpu_custom_call" | custom-call | flops 268435456 | bytes 1048576 | tf_op jit(solution)/shard_map/pallas_call | solution.py:326
  49.8 0.6 %dynamic_slice.4 = s32[1]{0:T(128)} dynamic-slice(s32[4]{0:T(128)S(1)} %copy-done.7, s32[]{:T(128)S(6)} %select_n.12), dynamic_slice_sizes={1} | dynamic-slice | bytes 12 | tf_op jit(solution)/shard_map/jit(dynamic_index_in_dim)/dynamic_slice | solution.py:364
  51.1 0.7 %broadcast_select_fusion = bf16[2,16,2048]{2,1,0:T(8,128)(2,1)} fusion(bf16[2,16,2048]{2,1,0:T(8,128)(2,1)S(1)} %shard_map.109, pred[]{:T(512)} %bitcast), kind=kLoop, calls=%fused_computation | loop fusion | flops 65536 | bytes 262145 | tf_op jit(solution)/shard_map/jit(_where)/select_n | solution.py:365
Async XLA Ops:
  0.0 3.1 %copy-start.7 = (s32[4]{0:T(128)S(1)}, s32[4]{0:T(128)}, u32[]{:S(2)}) copy-start(s32[4]{0:T(128)} %lens.1) | copy-start | bytes 52
  0.7 2.4 %copy-start = (bf16[2048,128]{1,0:T(8,128)(2,1)S(1)}, bf16[2048,128]{1,0:T(8,128)(2,1)}, u32[]{:S(2)}) copy-start(bf16[2048,128]{1,0:T(8,128)(2,1)} %wq.1) | copy-start | bytes 1572868
  0.7 2.4 %copy-start.1 = (bf16[128,2048]{1,0:T(8,128)(2,1)S(1)}, bf16[128,2048]{1,0:T(8,128)(2,1)}, u32[]{:S(2)}) copy-start(bf16[128,2048]{1,0:T(8,128)(2,1)} %wo.1) | copy-start | bytes 1572868
  1.9 1.2 %copy-start.2 = (bf16[2,16,2048]{2,1,0:T(8,128)(2,1)S(1)}, bf16[2,16,2048]{2,1,0:T(8,128)(2,1)}, u32[]{:S(2)}) copy-start(bf16[2,16,2048]{2,1,0:T(8,128)(2,1)} %hidden.1) | copy-start | bytes 393220
  3.1 0.9 %copy-start.3 = (f32[256,128]{1,0:T(8,128)S(1)}, f32[256,128]{1,0:T(8,128)}, u32[]{:S(2)}) copy-start(f32[256,128]{1,0:T(8,128)} %constant.27.clone.cosq) | copy-start | bytes 393220
  4.0 0.9 %copy-start.4 = (f32[256,128]{1,0:T(8,128)S(1)}, f32[256,128]{1,0:T(8,128)}, u32[]{:S(2)}) copy-start(f32[256,128]{1,0:T(8,128)} %constant.28.clone.sinq) | copy-start | bytes 393220
  4.9 0.8 %copy-start.5 = (f32[64,256]{1,0:T(8,128)S(1)}, f32[64,256]{1,0:T(8,128)}, u32[]{:S(2)}) copy-start(f32[64,256]{1,0:T(8,128)} %constant.29.clone.cosk) | copy-start | bytes 196612
  5.8 0.8 %copy-start.6 = (f32[64,256]{1,0:T(8,128)S(1)}, f32[64,256]{1,0:T(8,128)}, u32[]{:S(2)}) copy-start(f32[64,256]{1,0:T(8,128)} %constant.30.clone.sink) | copy-start | bytes 196612

commit v2 on v1

--- a/solution.py
+++ b/solution.py
@@ -116,15 +116,15 @@
     cosine, sine = np.cos(angles), np.sin(angles)
     wide_cos = np.concatenate([cosine, cosine], axis=1).astype(np.float32)
     wide_sin = np.concatenate([-sine, sine], axis=1).astype(np.float32)
-    return wide_cos, wide_sin, cosine.T.astype(np.float32), sine.T.astype(np.float32)
+    return np.stack([wide_cos, wide_sin]), np.stack([cosine.T, sine.T]).astype(np.float32)
 
 
 SWAP, GZ, GX, GY, GD, KV, RD, RX, RY, RZ, BACK, COUNT = 0, 1, 5, 9, 13, 17, 33, 37, 41, 45, 49, 50
 
 
 def span_kernel(
-    lens, hidden, gain, wq, wk, wv, wo, cosq, sinq, cosk, sink, out,
-    swap_buf, own_rows, x, wqv, wkn, wvn, wov, q, kv, heads, part, out_send, rd, rx, ry, rz, fin, fin_in,
+    lens, hidden, gain, wq, wk, wv, wo, wide_table, tall_table, out,
+    gain_rows, own_in, swap_buf, own_rows, x, wqv, wkv, wov, turn_q, turn_k, q, kv, heads, part, out_send, rd, rx, ry, rz, fin, fin_in,
     send, recv, local,
 ):
     d = lax.axis_index("dp")
@@ -142,12 +142,18 @@
     greeted = [sibling] + [chip(*peer) for peer in kv_peers] + [chip(2, 0), chip(3, 0)]
 
     loads = [
-        pltpu.make_async_copy(wk, wkn, local.at[0]),
-        pltpu.make_async_copy(wv, wvn, local.at[1]),
+        pltpu.make_async_copy(wk, wkv.at[0:16], local.at[0]),
+        pltpu.make_async_copy(wv, wkv.at[16:32], local.at[1]),
         pltpu.make_async_copy(wq, wqv, local.at[2]),
         pltpu.make_async_copy(wo, wov, local.at[3]),
+        pltpu.make_async_copy(wide_table, turn_q, local.at[4]),
+        pltpu.make_async_copy(tall_table, turn_k, local.at[5]),
     ]
-    for load in loads:
+    early = [
+        pltpu.make_async_copy(hidden.at[d], own_in, local.at[6]),
+        pltpu.make_async_copy(gain, gain_rows, local.at[7]),
+    ]
+    for load in early + loads:
         load.start()
 
     barrier = pltpu.get_barrier_semaphore()
@@ -174,8 +180,10 @@
     push(hidden.at[1 - d], swap_buf, SWAP, SWAP, sibling)
     busy = jnp.where(lens[0] > 0, 0, 1)
     length = jnp.where(busy == 0, lens[d], lens[2 + d])
+    for load in early:
+        load.wait()
     take(swap_buf, SWAP)
-    rows = jnp.where(busy == d, hidden[d].astype(jnp.float32), swap_buf[...].astype(jnp.float32))
+    rows = jnp.where(busy == d, own_in[...].astype(jnp.float32), swap_buf[...].astype(jnp.float32))
     own_rows[...] = rows
     scale = lax.rsqrt(jnp.mean(rows * rows, axis=-1, keepdims=True) + 1e-05)
 
@@ -185,7 +193,7 @@
     def block(ck, zk):
         return x.at[slot(ck, zk)]
 
-    x[slot(0, 0)] = (rows * scale * gain[...].astype(jnp.float32)).astype(jnp.bfloat16)
+    x[slot(0, 0)] = (rows * scale * gain_rows[...].astype(jnp.float32)[None, :]).astype(jnp.bfloat16)
 
     def spread(k):
         push(block(0, k), block(0, k), GX + k, GX + k, near_x)
@@ -222,10 +230,9 @@
     def project(half):
         lines = x[pl.ds(half * 8, 8)].reshape(128, x.shape[2])
         q[pl.ds(half * 128, 128), :] = jnp.dot(lines, wqv[...], preferred_element_type=jnp.float32).astype(jnp.bfloat16)
-        keys = jnp.dot(lines, wkn[...], preferred_element_type=jnp.float32)
-        values = jnp.dot(lines, wvn[...], preferred_element_type=jnp.float32)
-        kv[half, member, 0:16, :] = keys.T.astype(jnp.bfloat16)
-        kv[half, member, 16:32, :] = values.T.astype(jnp.bfloat16)
+        kv[half, member] = lax.dot_general(
+            wkv[...], lines, (((1,), (1,)), ((), ())), preferred_element_type=jnp.float32
+        ).astype(jnp.bfloat16)
         for k, peer in enumerate(kv_peers, 1):
             index = KV + half * 8 + k
             push(kv.at[half, member], kv.at[half, member], index, index, chip(*peer))
@@ -241,7 +248,7 @@
     project(1 - first)
 
     wide = q[...].astype(jnp.float32)
-    query = (wide * cosq[...] + pltpu.roll(wide, 64, 1) * sinq[...]).astype(jnp.bfloat16)
+    query = (wide * turn_q[0] + pltpu.roll(wide, 64, 1) * turn_q[1]).astype(jnp.bfloat16)
     for half in range(2):
         for k, (zk, ck) in enumerate(kv_peers, 1):
             take(kv.at[half, (zs[zk] % 2) * 4 + cs[ck]], KV + half * 8 + k)
@@ -252,7 +259,7 @@
     keys = joined(0).astype(jnp.float32)
     upper, lower = keys[:64], keys[64:]
     turned = jnp.concatenate(
-        [upper * cosk[...] - lower * sink[...], lower * cosk[...] + upper * sink[...]], axis=0
+        [upper * turn_k[0] - lower * turn_k[1], lower * turn_k[0] + upper * turn_k[1]], axis=0
     ).astype(jnp.bfloat16)
     scores = jnp.dot(query, turned, preferred_element_type=jnp.float32) * (1.0 / math.sqrt(128))
 
@@ -309,33 +316,37 @@
     ids = g * 16 + lax.broadcasted_iota(jnp.int32, total.shape, 0)
     fin[...] = jnp.where(ids < length, own_rows[...] + total, 0.0).astype(jnp.bfloat16)
     push(fin, fin_in, BACK, BACK, sibling)
-    out[d] = fin[...]
+    out[d] = jnp.where(busy == d, fin[...].astype(jnp.float32), 0.0).astype(jnp.bfloat16)
     take(fin_in, BACK)
-    out[1 - d] = fin_in[...]
+    out[1 - d] = jnp.where(busy == d, fin_in[...].astype(jnp.float32), 0.0).astype(jnp.bfloat16)
     for copy in started:
         copy.wait_send()
 
 
 def fused(hidden_in, span_lengths, norm_gain, query_weight, key_weight, value_weight, out_weight):
-    slots, rows, width = hidden_in.shape
+    _, rows, width = hidden_in.shape
     head_size = query_weight.shape[1]
     span = rows * 16
     vmem = pl.BlockSpec(memory_space=pltpu.VMEM)
-    anywhere = pl.BlockSpec(memory_space=pl.ANY)
+    hbm = pl.BlockSpec(memory_space=pltpu.HBM)
     bf16, f32 = jnp.bfloat16, jnp.float32
-    result = pl.pallas_call(
+    wide_table, tall_table = tables(span, head_size)
+    return pl.pallas_call(
         span_kernel,
         out_shape=jax.ShapeDtypeStruct(hidden_in.shape, bf16),
-        in_specs=[pl.BlockSpec(memory_space=pltpu.SMEM), vmem, vmem] + [anywhere] * 4 + [vmem] * 4,
+        in_specs=[pl.BlockSpec(memory_space=pltpu.SMEM)] + [hbm] * 8,
         out_specs=vmem,
         scratch_shapes=[
+            pltpu.VMEM((width,), bf16),
+            pltpu.VMEM((rows, width), bf16),
             pltpu.VMEM((rows, width), bf16),
             pltpu.VMEM((rows, width), f32),
             pltpu.VMEM((16, rows, width), bf16),
             pltpu.VMEM(query_weight.shape, bf16),
-            pltpu.VMEM(key_weight.shape, bf16),
-            pltpu.VMEM(value_weight.shape, bf16),
+            pltpu.VMEM((2 * key_weight.shape[1], width), bf16),
             pltpu.VMEM(out_weight.shape, bf16),
+            pltpu.VMEM(wide_table.shape, f32),
+            pltpu.VMEM(tall_table.shape, f32),
             pltpu.VMEM((span, head_size), bf16),
             pltpu.VMEM((2, 8, 32, 128), bf16),
             pltpu.VMEM((span, head_size), bf16),
@@ -349,20 +360,18 @@
             pltpu.VMEM((rows, width), bf16),
             pltpu.SemaphoreType.DMA((COUNT,)),
             pltpu.SemaphoreType.DMA((COUNT,)),
-            pltpu.SemaphoreType.DMA((4,)),
+            pltpu.SemaphoreType.DMA((8,)),
         ],
         compiler_params=pltpu.CompilerParams(
-            collective_id=0, has_side_effects=True, vmem_limit_bytes=32 * 1024 * 1024
+            collective_id=0, has_side_effects=True, vmem_limit_bytes=56 * 1024 * 1024
         ),
         cost_estimate=pl.CostEstimate(
             flops=4 * span * width * head_size, bytes_accessed=4 * width * head_size, transcendentals=span * span
         ),
     )(
-        span_lengths, hidden_in, norm_gain.reshape(1, width), query_weight, key_weight, value_weight,
-        out_weight, *tables(span, head_size),
-    )
-    holds = lax.dynamic_index_in_dim(span_lengths, lax.axis_index("dp") * slots, keepdims=False) > 0
-    return jnp.where(holds, result, jnp.zeros_like(result))
+        span_lengths, hidden_in, norm_gain, query_weight, key_weight.T, value_weight.T,
+        out_weight, wide_table, tall_table,
+    )
 
 
 def shards(hidden_in, span_lengths, norm_gain, query_weight, key_weight, value_weight, out_weight):

time: 52.1 us -> 45.6 us (0.88)
  local copies, waits for them, and re-layouts: 7.14 us -> 1.57 us
  between operations: 0.74 us -> 0.01 us
  Pallas kernels: 43.2 us -> 43.9 us
  other arithmetic: 0.67 us -> 0 us
    unnamed x18 -> x1, local copies, waits for them, and re-layouts: 5.84 us -> 1.57 us
    pallas_call x1, Pallas kernels: 43.2 us -> 43.9 us  [fused(): pl.pallas_call(span_kernel, out_shape=jax.ShapeDtypeStruct(hidden_in.shap...]
    reshape x1 -> x0, local copies, waits for them, and re-layouts: 0.71 us -> none  [fused(): norm_gain.reshape(1, width)]
    select_n x1 -> x0, other arithmetic: 0.67 us -> none  [fused(): return jnp.where(holds, result, jnp.zeros_like(result))]
    dynamic_slice x1 -> x0, local copies, waits for them, and re-layouts: 0.59 us -> none  [fused(): lax.dynamic_index_in_dim(span_lengths, lax.axis_index('dp') * slots, keep...]
where the time goes in v2:
time: 45.6 us; the launch traced here: 45.5 us
  Pallas kernels  43.9 us (96%)
  local copies, waits for them, and re-layouts  1.57 us (3%)
    pallas_call x1, Pallas kernels, fused(): pl.pallas_call(span_kernel, out_shape=jax.ShapeDtypeStruct(hidden_in.shap...  43.9 us
    unnamed x1, local copies, waits for them, and re-layouts  1.57 us

profile of v2, /device:TPU:0, one launch (start us, length us, event | category | flops | bytes accessed | tf_op | source)
XLA Modules:
  0.0 45.5 jit_solution(6177418644586094545)
XLA Ops:
  0.0 43.9 %shard_map.91 = bf16[2,16,2048]{2,1,0:T(8,128)(2,1)} custom-call(s32[4]{0:T(128)} %lens.1, bf16[2,16,2048]{2,1,0:T(8,128)(2,1)} %hidden.1, bf16[2048]{0:T(1024)(128)(2,1)} %gain.1, bf16[2048,128]{1,0:T(8,128)(2,1)} %wq.1, bf16[16,2048]{1,0:T(8,128)(2,1)} %bitcast.2, bf16[16,2048]{1,0:T(8,128)(2,1)} %bitcast.3, bf16[128,2048]{1,0:T(8,128)(2,1)} %wo.1, ...), custom_call_target="tpu_custom_call" | custom-call | flops 268435456 | bytes 1048576 | tf_op jit(solution)/shard_map/pallas_call | solution.py:334
  43.9 1.6 %copy.11 = bf16[2,16,2048]{2,1,0:T(8,128)(2,1)} copy(bf16[2,16,2048]{2,1,0:T(8,128)(2,1)} %shard_map.91) | data formatting | bytes 262144

commit v3 on v2

--- a/solution.py
+++ b/solution.py
@@ -106,7 +106,7 @@
 
 def slot_positions(count):
     at = np.arange(count)
-    return (at // 16 % 4) * 64 + (at // 64) * 16 + at % 16
+    return (at // 16 % 4) * 64 + (at // 64 % 2) * 32 + (at // 128) * 16 + at % 16
 
 
 def tables(span, width):
@@ -119,19 +119,21 @@
     return np.stack([wide_cos, wide_sin]), np.stack([cosine.T, sine.T]).astype(np.float32)
 
 
-SWAP, GZ, GX, GY, GD, KV, RD, RX, RY, RZ, BACK, COUNT = 0, 1, 5, 9, 13, 17, 33, 37, 41, 45, 49, 50
+SWAP, GZ, GY, KV, RY, RZ, BACK, WEIGHT, SHARE, COUNT = 0, 1, 5, 9, 17, 21, 25, 26, 30, 33
 
 
 def span_kernel(
     lens, hidden, gain, wq, wk, wv, wo, wide_table, tall_table, out,
-    gain_rows, own_in, swap_buf, own_rows, x, wqv, wkv, wov, turn_q, turn_k, q, kv, heads, part, out_send, rd, rx, ry, rz, fin, fin_in,
-    send, recv, local,
+    gain_rows, own_in, swap_buf, own_rows, x, wqv, wkv, wov, turn_q, turn_k,
+    query, kv, heads, part, out_send, ry, rz, fin, fin_in, send, recv, local,
 ):
     d = lax.axis_index("dp")
     g = lax.axis_index("group")
     z, c = g // 4, g % 4
+    y, plane = c // 2, c % 2
     zs = (z, z + 1 - 2 * (z % 2), (z + 2) % 4, 3 - z)
     cs = (c, c + 1 - 2 * (c % 2), (c + 2) % 4, 3 - c)
+    wide = x.shape[2]
 
     def chip(zk, ck):
         return {"group": zs[zk] * 4 + cs[ck]}
@@ -141,17 +143,23 @@
     kv_peers = [(k // 4, k % 4) for k in range(1, 8)]
     greeted = [sibling] + [chip(*peer) for peer in kv_peers] + [chip(2, 0), chip(3, 0)]
 
-    loads = [
-        pltpu.make_async_copy(wk, wkv.at[0:16], local.at[0]),
-        pltpu.make_async_copy(wv, wkv.at[16:32], local.at[1]),
-        pltpu.make_async_copy(wq, wqv, local.at[2]),
-        pltpu.make_async_copy(wo, wov, local.at[3]),
-        pltpu.make_async_copy(wide_table, turn_q, local.at[4]),
-        pltpu.make_async_copy(tall_table, turn_k, local.at[5]),
-    ]
+    def key_rows(at):
+        return wkv.at[pl.ds(at * 32, 16)], wkv.at[pl.ds(at * 32 + 16, 16)]
+
+    def out_rows(at, count=128, low=0):
+        return wov.at[pl.ds(at * 128 + low, count)]
+
     early = [
         pltpu.make_async_copy(hidden.at[d], own_in, local.at[6]),
         pltpu.make_async_copy(gain, gain_rows, local.at[7]),
+    ]
+    loads = [
+        pltpu.make_async_copy(wk, key_rows(plane)[0], local.at[0]),
+        pltpu.make_async_copy(wv, key_rows(plane)[1], local.at[1]),
+        pltpu.make_async_copy(wq, wqv.at[plane], local.at[2]),
+        pltpu.make_async_copy(wo, out_rows(plane), local.at[3]),
+        pltpu.make_async_copy(wide_table, turn_q, local.at[4]),
+        pltpu.make_async_copy(tall_table, turn_k, local.at[5]),
     ]
     for load in early + loads:
         load.start()
@@ -178,80 +186,81 @@
         ).wait_recv()
 
     push(hidden.at[1 - d], swap_buf, SWAP, SWAP, sibling)
+
+    half_q = pl.ds(d * (wide // 2), wide // 2)
+
+    def query_half(at):
+        return wqv.at[at, half_q]
+
+    def key_half(at, which):
+        return wkv.at[pl.ds(at * 32 + which * 16, 16), half_q]
+
+    def out_half(at):
+        return out_rows(at, 64, d * 64)
+
+    push(wq.at[half_q], query_half(plane), WEIGHT, WEIGHT, near_x)
+    push(wk.at[:, half_q], key_half(plane, 0), WEIGHT + 1, WEIGHT + 1, near_x)
+    push(wv.at[:, half_q], key_half(plane, 1), WEIGHT + 2, WEIGHT + 2, near_x)
+
+    for load in early:
+        load.wait()
     busy = jnp.where(lens[0] > 0, 0, 1)
     length = jnp.where(busy == 0, lens[d], lens[2 + d])
-    for load in early:
-        load.wait()
     take(swap_buf, SWAP)
     rows = jnp.where(busy == d, own_in[...].astype(jnp.float32), swap_buf[...].astype(jnp.float32))
     own_rows[...] = rows
     scale = lax.rsqrt(jnp.mean(rows * rows, axis=-1, keepdims=True) + 1e-05)
 
-    def slot(ck, zk):
-        return cs[ck] * 4 + zs[zk]
-
-    def block(ck, zk):
-        return x.at[slot(ck, zk)]
+    def slot(yk, zk):
+        return (1 - y if yk else y) * 4 + zs[zk]
+
+    def block(yk, zk):
+        return x.at[slot(yk, zk)]
 
     x[slot(0, 0)] = (rows * scale * gain_rows[...].astype(jnp.float32)[None, :]).astype(jnp.bfloat16)
 
-    def spread(k):
-        push(block(0, k), block(0, k), GX + k, GX + k, near_x)
+    for k in (3, 2, 1):
+        push(block(0, 0), block(0, 0), GZ + k, GZ + k, chip(k, 0))
+    push(block(0, 0), block(0, 0), GY, GY, near_y)
+    push(wo.at[pl.ds(d * 64, 64)], out_half(plane), WEIGHT + 3, WEIGHT + 3, near_x)
+    for k in (1, 2, 3):
+        take(block(0, k), GZ + k)
         push(block(0, k), block(0, k), GY + k, GY + k, near_y)
 
-    for k in (1, 2, 3):
-        push(block(0, 0), block(0, 0), GZ + k, GZ + k, chip(k, 0))
-    spread(0)
-
-    def relay(k):
-        if k % 2 == 0:
-            take(block(1, k), GX + k)
-            push(block(1, k), block(1, k), GD + k, GD + k, near_y)
-        else:
-            take(block(2, k), GY + k)
-            push(block(2, k), block(2, k), GD + k, GD + k, near_x)
-
-    take(block(0, 1), GZ + 1)
-    spread(1)
-    relay(0)
-    take(block(0, 2), GZ + 2)
-    spread(2)
-    relay(1)
-    take(block(0, 3), GZ + 3)
-    spread(3)
-    relay(2)
-    relay(3)
-
+    other = 1 - plane
+    take(query_half(other), WEIGHT)
+    push(query_half(other), query_half(other), SHARE, SHARE, sibling)
+    take(key_half(other, 0), WEIGHT + 1)
+    take(key_half(other, 1), WEIGHT + 2)
+    both = wkv.at[pl.ds(other * 32, 32), half_q]
+    push(both, both, SHARE + 1, SHARE + 1, sibling)
     for load in loads:
         load.wait()
-
-    member = g % 8
-
-    def project(half):
-        lines = x[pl.ds(half * 8, 8)].reshape(128, x.shape[2])
-        q[pl.ds(half * 128, 128), :] = jnp.dot(lines, wqv[...], preferred_element_type=jnp.float32).astype(jnp.bfloat16)
-        kv[half, member] = lax.dot_general(
-            wkv[...], lines, (((1,), (1,)), ((), ())), preferred_element_type=jnp.float32
-        ).astype(jnp.bfloat16)
-        for k, peer in enumerate(kv_peers, 1):
-            index = KV + half * 8 + k
-            push(kv.at[half, member], kv.at[half, member], index, index, chip(*peer))
-
-    first = c // 2
-    take(block(1, 1), GX + 1)
-    take(block(1, 3), GX + 3)
-    project(first)
-    take(block(2, 0), GY)
-    take(block(2, 2), GY + 2)
+    rest = pl.ds((1 - d) * (wide // 2), wide // 2)
+    take(wqv.at[other, rest], SHARE)
+    take(wkv.at[pl.ds(other * 32, 32), rest], SHARE + 1)
     for k in range(4):
-        take(block(3, k), GD + k)
-    project(1 - first)
-
-    wide = q[...].astype(jnp.float32)
-    query = (wide * turn_q[0] + pltpu.roll(wide, 64, 1) * turn_q[1]).astype(jnp.bfloat16)
-    for half in range(2):
-        for k, (zk, ck) in enumerate(kv_peers, 1):
-            take(kv.at[half, (zs[zk] % 2) * 4 + cs[ck]], KV + half * 8 + k)
+        take(block(1, k), GY + k)
+
+    lines = x[...].reshape(128, wide)
+    pair = (z % 2) * 2 + y
+    kv[plane, pl.ds(pair * 2, 2)] = (
+        lax.dot_general(wkv[...], lines, (((1,), (1,)), ((), ())), preferred_element_type=jnp.float32)
+        .astype(jnp.bfloat16)
+        .reshape(2, 32, 128)
+    )
+    own_kv = kv.at[plane, pl.ds(pair * 2, 2)]
+    for k, peer in enumerate(kv_peers, 1):
+        push(own_kv, own_kv, KV + k, KV + k, chip(*peer))
+    turn = (turn_q[0, pl.ds(plane * 128, 128), :], turn_q[1, pl.ds(plane * 128, 128), :])
+    for at in range(2):
+        plain = jnp.dot(lines, wqv[at], preferred_element_type=jnp.float32).astype(jnp.bfloat16).astype(jnp.float32)
+        query[at * 128 : at * 128 + 128, :] = (plain * turn[0] + pltpu.roll(plain, 64, 1) * turn[1]).astype(jnp.bfloat16)
+    take(out_half(other), WEIGHT + 3)
+    push(out_half(other), out_half(other), SHARE + 2, SHARE + 2, sibling)
+    for k, (zk, ck) in enumerate(kv_peers, 1):
+        theirs = (zs[zk] % 2) * 2 + cs[ck] // 2
+        take(kv.at[cs[ck] % 2, pl.ds(theirs * 2, 2)], KV + k)
 
     def joined(low):
         return jnp.concatenate([kv[half, :, low : low + 16, :].reshape(128, 128) for half in range(2)], axis=1)
@@ -261,50 +270,35 @@
     turned = jnp.concatenate(
         [upper * turn_k[0] - lower * turn_k[1], lower * turn_k[0] + upper * turn_k[1]], axis=0
     ).astype(jnp.bfloat16)
-    scores = jnp.dot(query, turned, preferred_element_type=jnp.float32) * (1.0 / math.sqrt(128))
+    scores = jnp.dot(query[...], turned, preferred_element_type=jnp.float32) * (1.0 / math.sqrt(128))
 
     def position(dim):
         at = lax.broadcasted_iota(jnp.int32, scores.shape, dim)
-        return ((at >> 4) & 3) * 64 + (at >> 6) * 16 + (at & 15)
-
-    scores = jnp.where(position(1) <= position(0), scores, -1e30)
+        return ((at >> 4) & 3) * 64 + ((at >> 6) & 1) * 32 + (at & 15), at >> 7
+
+    row_at, col_at = position(0)[0] + plane * 16, position(1)[0] + position(1)[1] * 16
+    scores = jnp.where(col_at <= row_at, scores, -1e30)
     expo = jnp.exp(scores - jnp.max(scores, axis=-1, keepdims=True))
     weights = (expo / jnp.sum(expo, axis=-1, keepdims=True)).astype(jnp.bfloat16)
-    heads[...] = lax.dot_general(
+    mixed = lax.dot_general(
         weights, joined(16), (((1,), (1,)), ((), ())), preferred_element_type=jnp.float32
     ).astype(jnp.bfloat16)
-
-    def partial(ck):
-        mine = heads[pl.ds(cs[ck] * 64, 64), :]
-        return jnp.dot(mine, wov[...], preferred_element_type=jnp.float32).reshape(4, 16, wov.shape[1])
-
-    out_send[pl.ds(cs[3] * 4, 4)] = partial(3).astype(jnp.bfloat16)
-    for k in (2, 3, 0, 1):
-        push(out_send.at[slot(3, k)], rd.at[k], RD + k, RD + k, near_x if k % 2 == 0 else near_y)
-    part[pl.ds(cs[1] * 4, 4)] = partial(1)
-    part[pl.ds(cs[2] * 4, 4)] = partial(2)
-
-    def hand_on(ck, k, with_relayed):
-        own = part[slot(ck, k)]
-        if with_relayed:
-            take(rd.at[k], RD + k)
-            own = own + rd[k].astype(jnp.float32)
-        out_send[slot(ck, k)] = own.astype(jnp.bfloat16)
-        if ck == 1:
-            push(out_send.at[slot(1, k)], rx.at[k], RX + k, RX + k, near_x)
-        else:
-            push(out_send.at[slot(2, k)], ry.at[k], RY + k, RY + k, near_y)
-
-    for k in (2, 3, 0, 1):
-        hand_on(1 if k % 2 == 0 else 2, k, False)
-    part[pl.ds(cs[0] * 4, 4)] = partial(0)
-    for k in (2, 3, 0, 1):
-        hand_on(2 if k % 2 == 0 else 1, k, True)
+    heads[:, 0:128] = mixed[0:128]
+    heads[:, 128:256] = mixed[128:256]
+    take(out_rows(other, 64, (1 - d) * 64), SHARE + 2)
+
+    def partial(at):
+        mine = heads[pl.ds(at * 64, 64), :]
+        return jnp.dot(mine, wov[...], preferred_element_type=jnp.float32).reshape(4, 16, wide)
+
+    out_send[pl.ds((1 - y) * 4, 4)] = partial(1 - y).astype(jnp.bfloat16)
+    for k in (2, 3, 1, 0):
+        push(out_send.at[slot(1, k)], ry.at[k], RY + k, RY + k, near_y)
+    part[...] = partial(y)
 
     def column_sum(k):
-        take(rx.at[k], RX + k)
         take(ry.at[k], RY + k)
-        return part[slot(0, k)] + rx[k].astype(jnp.float32) + ry[k].astype(jnp.float32)
+        return part[zs[k]] + ry[k].astype(jnp.float32)
 
     for k in (2, 3, 1):
         out_send[slot(0, k)] = column_sum(k).astype(jnp.bfloat16)
@@ -327,7 +321,6 @@
     _, rows, width = hidden_in.shape
     head_size = query_weight.shape[1]
     span = rows * 16
-    vmem = pl.BlockSpec(memory_space=pltpu.VMEM)
     hbm = pl.BlockSpec(memory_space=pltpu.HBM)
     bf16, f32 = jnp.bfloat16, jnp.float32
     wide_table, tall_table = tables(span, head_size)
@@ -335,25 +328,23 @@
         span_kernel,
         out_shape=jax.ShapeDtypeStruct(hidden_in.shape, bf16),
         in_specs=[pl.BlockSpec(memory_space=pltpu.SMEM)] + [hbm] * 8,
-        out_specs=vmem,
+        out_specs=pl.BlockSpec(memory_space=pltpu.VMEM),
         scratch_shapes=[
             pltpu.VMEM((width,), bf16),
             pltpu.VMEM((rows, width), bf16),
             pltpu.VMEM((rows, width), bf16),
             pltpu.VMEM((rows, width), f32),
-            pltpu.VMEM((16, rows, width), bf16),
-            pltpu.VMEM(query_weight.shape, bf16),
-            pltpu.VMEM((2 * key_weight.shape[1], width), bf16),
-            pltpu.VMEM(out_weight.shape, bf16),
+            pltpu.VMEM((8, rows, width), bf16),
+            pltpu.VMEM((2, width, head_size), bf16),
+            pltpu.VMEM((4 * key_weight.shape[1], width), bf16),
+            pltpu.VMEM((2 * head_size, width), bf16),
             pltpu.VMEM(wide_table.shape, f32),
             pltpu.VMEM(tall_table.shape, f32),
             pltpu.VMEM((span, head_size), bf16),
             pltpu.VMEM((2, 8, 32, 128), bf16),
-            pltpu.VMEM((span, head_size), bf16),
-            pltpu.VMEM((16, rows, width), f32),
-            pltpu.VMEM((16, rows, width), bf16),
-            pltpu.VMEM((4, rows, width), bf16),
-            pltpu.VMEM((4, rows, width), bf16),
+            pltpu.VMEM((span // 2, 2 * head_size), bf16),
+            pltpu.VMEM((4, rows, width), f32),
+            pltpu.VMEM((8, rows, width), bf16),
             pltpu.VMEM((4, rows, width), bf16),
             pltpu.VMEM((4, rows, width), bf16),
             pltpu.VMEM((rows, width), bf16),

time: 45.6 us -> 39.1 us (0.86)
  Pallas kernels: 43.9 us -> 37.4 us
    pallas_call x1, Pallas kernels: 43.9 us -> 37.4 us  [fused(): pl.pallas_call(span_kernel, out_shape=jax.ShapeDtypeStruct(hidden_in.shap...]
where the time goes in v3:
time: 39.1 us; the launch traced here: 39 us
  Pallas kernels  37.4 us (96%)
  local copies, waits for them, and re-layouts  1.57 us (4%)
    pallas_call x1, Pallas kernels, fused(): pl.pallas_call(span_kernel, out_shape=jax.ShapeDtypeStruct(hidden_in.shap...  37.4 us
    unnamed x1, local copies, waits for them, and re-layouts  1.57 us

profile of v3, /device:TPU:0, one launch (start us, length us, event | category | flops | bytes accessed | tf_op | source)
XLA Modules:
  0.0 39.0 jit_solution(10946444132574141797)
XLA Ops:
  0.0 37.4 %shard_map.91 = bf16[2,16,2048]{2,1,0:T(8,128)(2,1)} custom-call(s32[4]{0:T(128)} %lens.1, bf16[2,16,2048]{2,1,0:T(8,128)(2,1)} %hidden.1, bf16[2048]{0:T(1024)(128)(2,1)} %gain.1, bf16[2048,128]{1,0:T(8,128)(2,1)} %wq.1, bf16[16,2048]{1,0:T(8,128)(2,1)} %bitcast.2, bf16[16,2048]{1,0:T(8,128)(2,1)} %bitcast.3, bf16[128,2048]{1,0:T(8,128)(2,1)} %wo.1, ...), custom_call_target="tpu_custom_call" | custom-call | flops 268435456 | bytes 1048576 | tf_op jit(solution)/shard_map/pallas_call | solution.py:327
  37.4 1.6 %copy.11 = bf16[2,16,2048]{2,1,0:T(8,128)(2,1)} copy(bf16[2,16,2048]{2,1,0:T(8,128)(2,1)} %shard_map.91) | data formatting | bytes 262144

commit v4 on v3

--- a/solution.py
+++ b/solution.py
@@ -106,7 +106,7 @@
 
 def slot_positions(count):
     at = np.arange(count)
-    return (at // 16 % 4) * 64 + (at // 64 % 2) * 32 + (at // 128) * 16 + at % 16
+    return (at // 16 % 4) * 64 + (at // 64) * 16 + at % 16
 
 
 def tables(span, width):
@@ -116,21 +116,19 @@
     cosine, sine = np.cos(angles), np.sin(angles)
     wide_cos = np.concatenate([cosine, cosine], axis=1).astype(np.float32)
     wide_sin = np.concatenate([-sine, sine], axis=1).astype(np.float32)
-    return np.stack([wide_cos, wide_sin]), np.stack([cosine.T, sine.T]).astype(np.float32)
-
-
-SWAP, GZ, GY, KV, RY, RZ, BACK, WEIGHT, SHARE, COUNT = 0, 1, 5, 9, 17, 21, 25, 26, 30, 33
+    return np.stack([wide_cos, wide_sin])
+
+
+SWAP, GZ, KV, RZ, BACK, FROM_X, FROM_Y, CROSS_X, CROSS_Y, SHARE, COUNT = 0, 1, 5, 13, 17, 18, 22, 26, 30, 34, 46
 
 
 def span_kernel(
-    lens, hidden, gain, wq, wk, wv, wo, wide_table, tall_table, out,
-    gain_rows, own_in, swap_buf, own_rows, x, wqv, wkv, wov, turn_q, turn_k,
-    query, kv, heads, part, out_send, ry, rz, fin, fin_in, send, recv, local,
+    lens, hidden, gain, wq, wk, wv, wo, table, out,
+    gain_rows, own_in, swap_buf, own_rows, x, wqv, wkv, wov, turn, query, kv, heads, part, out_send, rz, fin, fin_in, send, recv, local,
 ):
     d = lax.axis_index("dp")
     g = lax.axis_index("group")
     z, c = g // 4, g % 4
-    y, plane = c // 2, c % 2
     zs = (z, z + 1 - 2 * (z % 2), (z + 2) % 4, 3 - z)
     cs = (c, c + 1 - 2 * (c % 2), (c + 2) % 4, 3 - c)
     wide = x.shape[2]
@@ -142,24 +140,17 @@
     sibling = {"dp": 1 - d}
     kv_peers = [(k // 4, k % 4) for k in range(1, 8)]
     greeted = [sibling] + [chip(*peer) for peer in kv_peers] + [chip(2, 0), chip(3, 0)]
-
-    def key_rows(at):
-        return wkv.at[pl.ds(at * 32, 16)], wkv.at[pl.ds(at * 32 + 16, 16)]
-
-    def out_rows(at, count=128, low=0):
-        return wov.at[pl.ds(at * 128 + low, count)]
 
     early = [
         pltpu.make_async_copy(hidden.at[d], own_in, local.at[6]),
         pltpu.make_async_copy(gain, gain_rows, local.at[7]),
     ]
     loads = [
-        pltpu.make_async_copy(wk, key_rows(plane)[0], local.at[0]),
-        pltpu.make_async_copy(wv, key_rows(plane)[1], local.at[1]),
-        pltpu.make_async_copy(wq, wqv.at[plane], local.at[2]),
-        pltpu.make_async_copy(wo, out_rows(plane), local.at[3]),
-        pltpu.make_async_copy(wide_table, turn_q, local.at[4]),
-        pltpu.make_async_copy(tall_table, turn_k, local.at[5]),
+        pltpu.make_async_copy(wk, wkv.at[pl.ds(c * 16, 16)], local.at[0]),
+        pltpu.make_async_copy(wv, wkv.at[pl.ds(64 + c * 16, 16)], local.at[1]),
+        pltpu.make_async_copy(wq, wqv.at[c], local.at[2]),
+        pltpu.make_async_copy(wo, wov.at[pl.ds(c * 128, 128)], local.at[3]),
+        pltpu.make_async_copy(table, turn, local.at[4]),
     ]
     for load in early + loads:
         load.start()
@@ -187,20 +178,50 @@
 
     push(hidden.at[1 - d], swap_buf, SWAP, SWAP, sibling)
 
-    half_q = pl.ds(d * (wide // 2), wide // 2)
-
-    def query_half(at):
-        return wqv.at[at, half_q]
-
-    def key_half(at, which):
-        return wkv.at[pl.ds(at * 32 + which * 16, 16), half_q]
-
-    def out_half(at):
-        return out_rows(at, 64, d * 64)
-
-    push(wq.at[half_q], query_half(plane), WEIGHT, WEIGHT, near_x)
-    push(wk.at[:, half_q], key_half(plane, 0), WEIGHT + 1, WEIGHT + 1, near_x)
-    push(wv.at[:, half_q], key_half(plane, 1), WEIGHT + 2, WEIGHT + 2, near_x)
+    deep = wide // 2
+
+    def piece(which, ck, core, low=0, count=2):
+        quarter = deep // 2
+        if which == 0:
+            return wqv.at[cs[ck], pl.ds(core * deep + low * quarter, count * quarter)]
+        if which == 3:
+            return wov.at[pl.ds(cs[ck] * 128 + core * 64 + low * 32, count * 32)]
+        return wkv.at[pl.ds((which - 1) * 64 + cs[ck] * 16, 16), pl.ds(core * deep, deep)]
+
+    sources = (
+        wq.at[pl.ds(d * deep, deep)], wk.at[:, pl.ds(d * deep, deep)], wv.at[:, pl.ds(d * deep, deep)],
+        wo.at[pl.ds(d * 64, 64)],
+    )
+
+    def give(which):
+        push(sources[which], piece(which, 0, d), FROM_X + which, FROM_X + which, near_x)
+        push(sources[which], piece(which, 0, d), FROM_Y + which, FROM_Y + which, near_y)
+
+    def share(which, ck):
+        index = SHARE + (ck - 1) * 4 + which
+        push(piece(which, ck, d), piece(which, ck, d), index, index, sibling)
+
+    def pass_on(which):
+        take(piece(which, 1, d), FROM_X + which)
+        push(piece(which, 1, d, 0, 1), piece(which, 1, d, 0, 1), CROSS_X + which, CROSS_X + which, near_y)
+        take(piece(which, 2, d), FROM_Y + which)
+        push(piece(which, 2, d, 1, 1), piece(which, 2, d, 1, 1), CROSS_Y + which, CROSS_Y + which, near_x)
+        share(which, 1)
+        share(which, 2)
+
+    def across(which):
+        take(piece(which, 3, d, 0, 1), CROSS_X + which)
+        take(piece(which, 3, d, 1, 1), CROSS_Y + which)
+        share(which, 3)
+
+    def shared(which):
+        for ck in (1, 2, 3):
+            take(piece(which, ck, 1 - d), SHARE + (ck - 1) * 4 + which)
+
+    give(0)
+    for which in (1, 2):
+        give(which)
+        push(sources[which], piece(which, 0, d), CROSS_X + which, CROSS_X + which, chip(0, 3))
 
     for load in early:
         load.wait()
@@ -211,99 +232,70 @@
     own_rows[...] = rows
     scale = lax.rsqrt(jnp.mean(rows * rows, axis=-1, keepdims=True) + 1e-05)
 
-    def slot(yk, zk):
-        return (1 - y if yk else y) * 4 + zs[zk]
-
-    def block(yk, zk):
-        return x.at[slot(yk, zk)]
-
-    x[slot(0, 0)] = (rows * scale * gain_rows[...].astype(jnp.float32)[None, :]).astype(jnp.bfloat16)
+    x[z] = (rows * scale * gain_rows[...].astype(jnp.float32)[None, :]).astype(jnp.bfloat16)
 
     for k in (3, 2, 1):
-        push(block(0, 0), block(0, 0), GZ + k, GZ + k, chip(k, 0))
-    push(block(0, 0), block(0, 0), GY, GY, near_y)
-    push(wo.at[pl.ds(d * 64, 64)], out_half(plane), WEIGHT + 3, WEIGHT + 3, near_x)
-    for k in (1, 2, 3):
-        take(block(0, k), GZ + k)
-        push(block(0, k), block(0, k), GY + k, GY + k, near_y)
-
-    other = 1 - plane
-    take(query_half(other), WEIGHT)
-    push(query_half(other), query_half(other), SHARE, SHARE, sibling)
-    take(key_half(other, 0), WEIGHT + 1)
-    take(key_half(other, 1), WEIGHT + 2)
-    both = wkv.at[pl.ds(other * 32, 32), half_q]
-    push(both, both, SHARE + 1, SHARE + 1, sibling)
+        push(x.at[z], x.at[z], GZ + k, GZ + k, chip(k, 0))
+    pass_on(0)
+    give(3)
+    for which in (1, 2):
+        take(piece(which, 1, d), FROM_X + which)
+        take(piece(which, 2, d), FROM_Y + which)
+        take(piece(which, 3, d), CROSS_X + which)
+        for ck in (1, 2, 3):
+            share(which, ck)
     for load in loads:
         load.wait()
-    rest = pl.ds((1 - d) * (wide // 2), wide // 2)
-    take(wqv.at[other, rest], SHARE)
-    take(wkv.at[pl.ds(other * 32, 32), rest], SHARE + 1)
-    for k in range(4):
-        take(block(1, k), GY + k)
-
-    lines = x[...].reshape(128, wide)
-    pair = (z % 2) * 2 + y
-    kv[plane, pl.ds(pair * 2, 2)] = (
-        lax.dot_general(wkv[...], lines, (((1,), (1,)), ((), ())), preferred_element_type=jnp.float32)
-        .astype(jnp.bfloat16)
-        .reshape(2, 32, 128)
-    )
-    own_kv = kv.at[plane, pl.ds(pair * 2, 2)]
+    for k in (1, 2, 3):
+        take(x.at[zs[k]], GZ + k)
+    shared(1)
+    shared(2)
+
+    lines = x[...].reshape(64, wide)
+    kv[c, z % 2] = lax.dot_general(
+        lines, wkv[...], (((1,), (1,)), ((), ())), preferred_element_type=jnp.float32
+    ).astype(jnp.bfloat16)
+    own_kv = kv.at[c, z % 2]
     for k, peer in enumerate(kv_peers, 1):
         push(own_kv, own_kv, KV + k, KV + k, chip(*peer))
-    turn = (turn_q[0, pl.ds(plane * 128, 128), :], turn_q[1, pl.ds(plane * 128, 128), :])
-    for at in range(2):
+    across(0)
+    shared(0)
+    cosine, sine = turn[0, pl.ds(c * 64, 64), :], turn[1, pl.ds(c * 64, 64), :]
+    for at in range(4):
         plain = jnp.dot(lines, wqv[at], preferred_element_type=jnp.float32).astype(jnp.bfloat16).astype(jnp.float32)
-        query[at * 128 : at * 128 + 128, :] = (plain * turn[0] + pltpu.roll(plain, 64, 1) * turn[1]).astype(jnp.bfloat16)
-    take(out_half(other), WEIGHT + 3)
-    push(out_half(other), out_half(other), SHARE + 2, SHARE + 2, sibling)
+        query[at * 64 : at * 64 + 64, :] = (plain * cosine + pltpu.roll(plain, 64, 1) * sine).astype(jnp.bfloat16)
     for k, (zk, ck) in enumerate(kv_peers, 1):
-        theirs = (zs[zk] % 2) * 2 + cs[ck] // 2
-        take(kv.at[cs[ck] % 2, pl.ds(theirs * 2, 2)], KV + k)
+        take(kv.at[cs[ck], zs[zk] % 2], KV + k)
+    pass_on(3)
 
     def joined(low):
-        return jnp.concatenate([kv[half, :, low : low + 16, :].reshape(128, 128) for half in range(2)], axis=1)
+        return jnp.concatenate([kv[:, half, :, low : low + 64].reshape(256, 64) for half in range(2)], axis=1)
 
     keys = joined(0).astype(jnp.float32)
-    upper, lower = keys[:64], keys[64:]
-    turned = jnp.concatenate(
-        [upper * turn_k[0] - lower * turn_k[1], lower * turn_k[0] + upper * turn_k[1]], axis=0
-    ).astype(jnp.bfloat16)
-    scores = jnp.dot(query[...], turned, preferred_element_type=jnp.float32) * (1.0 / math.sqrt(128))
+    turned = (keys * turn[0] + pltpu.roll(keys, 64, 1) * turn[1]).astype(jnp.bfloat16)
+    scores = lax.dot_general(
+        query[...], turned, (((1,), (1,)), ((), ())), preferred_element_type=jnp.float32
+    ) * (1.0 / math.sqrt(128))
 
     def position(dim):
         at = lax.broadcasted_iota(jnp.int32, scores.shape, dim)
-        return ((at >> 4) & 3) * 64 + ((at >> 6) & 1) * 32 + (at & 15), at >> 7
-
-    row_at, col_at = position(0)[0] + plane * 16, position(1)[0] + position(1)[1] * 16
+        return ((at >> 4) & 3) * 64 + (at & 15), at >> 6
+
+    row_at, col_at = position(0)[0] + c * 16, position(1)[0] + position(1)[1] * 16
     scores = jnp.where(col_at <= row_at, scores, -1e30)
     expo = jnp.exp(scores - jnp.max(scores, axis=-1, keepdims=True))
     weights = (expo / jnp.sum(expo, axis=-1, keepdims=True)).astype(jnp.bfloat16)
-    mixed = lax.dot_general(
-        weights, joined(16), (((1,), (1,)), ((), ())), preferred_element_type=jnp.float32
-    ).astype(jnp.bfloat16)
-    heads[:, 0:128] = mixed[0:128]
-    heads[:, 128:256] = mixed[128:256]
-    take(out_rows(other, 64, (1 - d) * 64), SHARE + 2)
-
-    def partial(at):
-        mine = heads[pl.ds(at * 64, 64), :]
-        return jnp.dot(mine, wov[...], preferred_element_type=jnp.float32).reshape(4, 16, wide)
-
-    out_send[pl.ds((1 - y) * 4, 4)] = partial(1 - y).astype(jnp.bfloat16)
-    for k in (2, 3, 1, 0):
-        push(out_send.at[slot(1, k)], ry.at[k], RY + k, RY + k, near_y)
-    part[...] = partial(y)
-
-    def column_sum(k):
-        take(ry.at[k], RY + k)
-        return part[zs[k]] + ry[k].astype(jnp.float32)
-
+    mixed = jnp.dot(weights, joined(64), preferred_element_type=jnp.float32).astype(jnp.bfloat16)
+    for at in range(4):
+        heads[:, at * 128 : at * 128 + 128] = mixed[at * 64 : at * 64 + 64]
+    across(3)
+    shared(3)
+
+    part[...] = jnp.dot(heads[...], wov[...], preferred_element_type=jnp.float32).reshape(4, 16, wide)
     for k in (2, 3, 1):
-        out_send[slot(0, k)] = column_sum(k).astype(jnp.bfloat16)
-        push(out_send.at[slot(0, k)], rz.at[k], RZ + k, RZ + k, chip(k, 0))
-    total = column_sum(0)
+        out_send[zs[k]] = part[zs[k]].astype(jnp.bfloat16)
+        push(out_send.at[zs[k]], rz.at[k], RZ + k, RZ + k, chip(k, 0))
+    total = part[z]
     for k in (2, 3, 1):
         take(rz.at[k], RZ + k)
         total = total + rz[k].astype(jnp.float32)
@@ -323,28 +315,26 @@
     span = rows * 16
     hbm = pl.BlockSpec(memory_space=pltpu.HBM)
     bf16, f32 = jnp.bfloat16, jnp.float32
-    wide_table, tall_table = tables(span, head_size)
+    table = tables(span, head_size)
     return pl.pallas_call(
         span_kernel,
         out_shape=jax.ShapeDtypeStruct(hidden_in.shape, bf16),
-        in_specs=[pl.BlockSpec(memory_space=pltpu.SMEM)] + [hbm] * 8,
+        in_specs=[pl.BlockSpec(memory_space=pltpu.SMEM)] + [hbm] * 7,
         out_specs=pl.BlockSpec(memory_space=pltpu.VMEM),
         scratch_shapes=[
             pltpu.VMEM((width,), bf16),
             pltpu.VMEM((rows, width), bf16),
             pltpu.VMEM((rows, width), bf16),
             pltpu.VMEM((rows, width), f32),
-            pltpu.VMEM((8, rows, width), bf16),
-            pltpu.VMEM((2, width, head_size), bf16),
-            pltpu.VMEM((4 * key_weight.shape[1], width), bf16),
-            pltpu.VMEM((2 * head_size, width), bf16),
-            pltpu.VMEM(wide_table.shape, f32),
-            pltpu.VMEM(tall_table.shape, f32),
+            pltpu.VMEM((4, rows, width), bf16),
+            pltpu.VMEM((4, width, head_size), bf16),
+            pltpu.VMEM((8 * key_weight.shape[1], width), bf16),
+            pltpu.VMEM((4 * head_size, width), bf16),
+            pltpu.VMEM(table.shape, f32),
             pltpu.VMEM((span, head_size), bf16),
-            pltpu.VMEM((2, 8, 32, 128), bf16),
-            pltpu.VMEM((span // 2, 2 * head_size), bf16),
+            pltpu.VMEM((4, 2, 64, 128), bf16),
+            pltpu.VMEM((span // 4, 4 * head_size), bf16),
             pltpu.VMEM((4, rows, width), f32),
-            pltpu.VMEM((8, rows, width), bf16),
             pltpu.VMEM((4, rows, width), bf16),
             pltpu.VMEM((4, rows, width), bf16),
             pltpu.VMEM((rows, width), bf16),
@@ -361,7 +351,7 @@
         ),
     )(
         span_lengths, hidden_in, norm_gain, query_weight, key_weight.T, value_weight.T,
-        out_weight, wide_table, tall_table,
+        out_weight, table,
     )
 
 

time: 39.1 us -> 42.5 us (1.087)
  Pallas kernels: 37.4 us -> 40.8 us
    pallas_call x1, Pallas kernels: 37.4 us -> 40.8 us  [fused(): pl.pallas_call(span_kernel, out_shape=jax.ShapeDtypeStruct(hidden_in.shap...]
where the time goes in v4:
time: 42.5 us; the launch traced here: 42.4 us
  Pallas kernels  40.8 us (96%)
  local copies, waits for them, and re-layouts  1.57 us (4%)
    pallas_call x1, Pallas kernels, fused(): pl.pallas_call(span_kernel, out_shape=jax.ShapeDtypeStruct(hidden_in.shap...  40.8 us
    unnamed x1, local copies, waits for them, and re-layouts  1.57 us

profile of v4, /device:TPU:0, one launch (start us, length us, event | category | flops | bytes accessed | tf_op | source)
XLA Modules:
  0.0 42.4 jit_solution(6908285515705817349)
XLA Ops:
  0.0 40.8 %shard_map.82 = bf16[2,16,2048]{2,1,0:T(8,128)(2,1)} custom-call(s32[4]{0:T(128)} %lens.1, bf16[2,16,2048]{2,1,0:T(8,128)(2,1)} %hidden.1, bf16[2048]{0:T(1024)(128)(2,1)} %gain.1, bf16[2048,128]{1,0:T(8,128)(2,1)} %wq.1, bf16[16,2048]{1,0:T(8,128)(2,1)} %bitcast.2, bf16[16,2048]{1,0:T(8,128)(2,1)} %bitcast.3, bf16[128,2048]{1,0:T(8,128)(2,1)} %wo.1, ...), custom_call_target="tpu_custom_call" | custom-call | flops 268435456 | bytes 1048576 | tf_op jit(solution)/shard_map/pallas_call | solution.py:319
  40.8 1.6 %copy.10 = bf16[2,16,2048]{2,1,0:T(8,128)(2,1)} copy(bf16[2,16,2048]{2,1,0:T(8,128)(2,1)} %shard_map.82) | data formatting | bytes 262144

commit v5 on v3

--- a/solution.py
+++ b/solution.py
@@ -106,7 +106,7 @@
 
 def slot_positions(count):
     at = np.arange(count)
-    return (at // 16 % 4) * 64 + (at // 64 % 2) * 32 + (at // 128) * 16 + at % 16
+    return (at // 16 % 2) * 128 + (at // 128) * 64 + (at // 32 % 4) * 16 + at % 16
 
 
 def tables(span, width):
@@ -119,18 +119,18 @@
     return np.stack([wide_cos, wide_sin]), np.stack([cosine.T, sine.T]).astype(np.float32)
 
 
-SWAP, GZ, GY, KV, RY, RZ, BACK, WEIGHT, SHARE, COUNT = 0, 1, 5, 9, 17, 21, 25, 26, 30, 33
+SWAP, GZ, GX, GY, GD, KV, RD, RX, RY, RZ, BACK, WEIGHT, SHARE, COUNT = 0, 1, 2, 4, 6, 8, 16, 18, 20, 22, 23, 24, 28, 31
 
 
 def span_kernel(
     lens, hidden, gain, wq, wk, wv, wo, wide_table, tall_table, out,
     gain_rows, own_in, swap_buf, own_rows, x, wqv, wkv, wov, turn_q, turn_k,
-    query, kv, heads, part, out_send, ry, rz, fin, fin_in, send, recv, local,
+    query, kv, heads, part, out_send, rd, rx, ry, rz, fin, fin_in, send, recv, local,
 ):
     d = lax.axis_index("dp")
     g = lax.axis_index("group")
     z, c = g // 4, g % 4
-    y, plane = c // 2, c % 2
+    plane, mine_z = z % 2, z // 2
     zs = (z, z + 1 - 2 * (z % 2), (z + 2) % 4, 3 - z)
     cs = (c, c + 1 - 2 * (c % 2), (c + 2) % 4, 3 - c)
     wide = x.shape[2]
@@ -138,10 +138,10 @@
     def chip(zk, ck):
         return {"group": zs[zk] * 4 + cs[ck]}
 
-    near_x, near_y = chip(0, 1), chip(0, 2)
+    near_x, near_y, partner, far = chip(0, 1), chip(0, 2), chip(1, 0), chip(2, 0)
     sibling = {"dp": 1 - d}
     kv_peers = [(k // 4, k % 4) for k in range(1, 8)]
-    greeted = [sibling] + [chip(*peer) for peer in kv_peers] + [chip(2, 0), chip(3, 0)]
+    greeted = [sibling] + [chip(*peer) for peer in kv_peers] + [far]
 
     def key_rows(at):
         return wkv.at[pl.ds(at * 32, 16)], wkv.at[pl.ds(at * 32 + 16, 16)]
@@ -198,9 +198,9 @@
     def out_half(at):
         return out_rows(at, 64, d * 64)
 
-    push(wq.at[half_q], query_half(plane), WEIGHT, WEIGHT, near_x)
-    push(wk.at[:, half_q], key_half(plane, 0), WEIGHT + 1, WEIGHT + 1, near_x)
-    push(wv.at[:, half_q], key_half(plane, 1), WEIGHT + 2, WEIGHT + 2, near_x)
+    push(wq.at[half_q], query_half(plane), WEIGHT, WEIGHT, partner)
+    push(wk.at[:, half_q], key_half(plane, 0), WEIGHT + 1, WEIGHT + 1, partner)
+    push(wv.at[:, half_q], key_half(plane, 1), WEIGHT + 2, WEIGHT + 2, partner)
 
     for load in early:
         load.wait()
@@ -211,21 +211,27 @@
     own_rows[...] = rows
     scale = lax.rsqrt(jnp.mean(rows * rows, axis=-1, keepdims=True) + 1e-05)
 
-    def slot(yk, zk):
-        return (1 - y if yk else y) * 4 + zs[zk]
-
-    def block(yk, zk):
-        return x.at[slot(yk, zk)]
+    def slot(ck, k):
+        return cs[ck] * 2 + (1 - mine_z if k else mine_z)
+
+    def block(ck, k):
+        return x.at[slot(ck, k)]
 
     x[slot(0, 0)] = (rows * scale * gain_rows[...].astype(jnp.float32)[None, :]).astype(jnp.bfloat16)
 
-    for k in (3, 2, 1):
-        push(block(0, 0), block(0, 0), GZ + k, GZ + k, chip(k, 0))
-    push(block(0, 0), block(0, 0), GY, GY, near_y)
-    push(wo.at[pl.ds(d * 64, 64)], out_half(plane), WEIGHT + 3, WEIGHT + 3, near_x)
-    for k in (1, 2, 3):
-        take(block(0, k), GZ + k)
+    def spread(k):
+        push(block(0, k), block(0, k), GX + k, GX + k, near_x)
         push(block(0, k), block(0, k), GY + k, GY + k, near_y)
+
+    push(block(0, 0), block(0, 0), GZ, GZ, far)
+    spread(0)
+    push(wo.at[pl.ds(d * 64, 64)], out_half(plane), WEIGHT + 3, WEIGHT + 3, partner)
+    take(block(0, 1), GZ)
+    spread(1)
+    take(block(1, 0), GX)
+    push(block(1, 0), block(1, 0), GD, GD, near_y)
+    take(block(2, 1), GY + 1)
+    push(block(2, 1), block(2, 1), GD + 1, GD + 1, near_x)
 
     other = 1 - plane
     take(query_half(other), WEIGHT)
@@ -239,17 +245,18 @@
     rest = pl.ds((1 - d) * (wide // 2), wide // 2)
     take(wqv.at[other, rest], SHARE)
     take(wkv.at[pl.ds(other * 32, 32), rest], SHARE + 1)
-    for k in range(4):
-        take(block(1, k), GY + k)
+    take(block(1, 1), GX + 1)
+    take(block(2, 0), GY)
+    for k in range(2):
+        take(block(3, k), GD + k)
 
     lines = x[...].reshape(128, wide)
-    pair = (z % 2) * 2 + y
-    kv[plane, pl.ds(pair * 2, 2)] = (
+    kv[plane, c] = (
         lax.dot_general(wkv[...], lines, (((1,), (1,)), ((), ())), preferred_element_type=jnp.float32)
         .astype(jnp.bfloat16)
         .reshape(2, 32, 128)
     )
-    own_kv = kv.at[plane, pl.ds(pair * 2, 2)]
+    own_kv = kv.at[plane, c]
     for k, peer in enumerate(kv_peers, 1):
         push(own_kv, own_kv, KV + k, KV + k, chip(*peer))
     turn = (turn_q[0, pl.ds(plane * 128, 128), :], turn_q[1, pl.ds(plane * 128, 128), :])
@@ -259,11 +266,15 @@
     take(out_half(other), WEIGHT + 3)
     push(out_half(other), out_half(other), SHARE + 2, SHARE + 2, sibling)
     for k, (zk, ck) in enumerate(kv_peers, 1):
-        theirs = (zs[zk] % 2) * 2 + cs[ck] // 2
-        take(kv.at[cs[ck] % 2, pl.ds(theirs * 2, 2)], KV + k)
+        take(kv.at[zs[zk] % 2, cs[ck]], KV + k)
 
     def joined(low):
-        return jnp.concatenate([kv[half, :, low : low + 16, :].reshape(128, 128) for half in range(2)], axis=1)
+        def part_of(half, bit):
+            return kv[half, :, bit, low : low + 16, :].reshape(64, 128)
+
+        return jnp.concatenate(
+            [jnp.concatenate([part_of(half, 0), part_of(half, 1)], axis=0) for half in range(2)], axis=1
+        )
 
     keys = joined(0).astype(jnp.float32)
     upper, lower = keys[:64], keys[64:]
@@ -274,9 +285,9 @@
 
     def position(dim):
         at = lax.broadcasted_iota(jnp.int32, scores.shape, dim)
-        return ((at >> 4) & 3) * 64 + ((at >> 6) & 1) * 32 + (at & 15), at >> 7
-
-    row_at, col_at = position(0)[0] + plane * 16, position(1)[0] + position(1)[1] * 16
+        return ((at >> 4) & 1) * 128 + ((at >> 5) & 3) * 16 + (at & 15), at >> 7
+
+    row_at, col_at = position(0)[0] + plane * 64, position(1)[0] + position(1)[1] * 64
     scores = jnp.where(col_at <= row_at, scores, -1e30)
     expo = jnp.exp(scores - jnp.max(scores, axis=-1, keepdims=True))
     weights = (expo / jnp.sum(expo, axis=-1, keepdims=True)).astype(jnp.bfloat16)
@@ -287,26 +298,43 @@
     heads[:, 128:256] = mixed[128:256]
     take(out_rows(other, 64, (1 - d) * 64), SHARE + 2)
 
-    def partial(at):
-        mine = heads[pl.ds(at * 64, 64), :]
-        return jnp.dot(mine, wov[...], preferred_element_type=jnp.float32).reshape(4, 16, wide)
-
-    out_send[pl.ds((1 - y) * 4, 4)] = partial(1 - y).astype(jnp.bfloat16)
-    for k in (2, 3, 1, 0):
-        push(out_send.at[slot(1, k)], ry.at[k], RY + k, RY + k, near_y)
-    part[...] = partial(y)
+    def partial(ck):
+        mine = heads[pl.ds(cs[ck] * 32, 32), :]
+        return jnp.dot(mine, wov[...], preferred_element_type=jnp.float32).reshape(2, 16, wide)
+
+    out_send[pl.ds(cs[3] * 2, 2)] = partial(3).astype(jnp.bfloat16)
+    push(out_send.at[slot(3, 1)], rd.at[1], RD + 1, RD + 1, near_y)
+    push(out_send.at[slot(3, 0)], rd.at[0], RD, RD, near_x)
+    part[pl.ds(cs[2] * 2, 2)] = partial(2)
+    part[pl.ds(cs[1] * 2, 2)] = partial(1)
+
+    def hand_on(ck, k, with_relayed):
+        own = part[slot(ck, k)]
+        if with_relayed:
+            take(rd.at[k], RD + k)
+            own = own + rd[k].astype(jnp.float32)
+        out_send[slot(ck, k)] = own.astype(jnp.bfloat16)
+        if ck == 1:
+            push(out_send.at[slot(1, k)], rx.at[k], RX + k, RX + k, near_x)
+        else:
+            push(out_send.at[slot(2, k)], ry.at[k], RY + k, RY + k, near_y)
+
+    hand_on(2, 1, False)
+    hand_on(1, 0, False)
+    part[pl.ds(cs[0] * 2, 2)] = partial(0)
+    hand_on(1, 1, True)
+    hand_on(2, 0, True)
 
     def column_sum(k):
+        take(rx.at[k], RX + k)
         take(ry.at[k], RY + k)
-        return part[zs[k]] + ry[k].astype(jnp.float32)
-
-    for k in (2, 3, 1):
-        out_send[slot(0, k)] = column_sum(k).astype(jnp.bfloat16)
-        push(out_send.at[slot(0, k)], rz.at[k], RZ + k, RZ + k, chip(k, 0))
+        return part[slot(0, k)] + rx[k].astype(jnp.float32) + ry[k].astype(jnp.float32)
+
+    out_send[slot(0, 1)] = column_sum(1).astype(jnp.bfloat16)
+    push(out_send.at[slot(0, 1)], rz, RZ, RZ, far)
     total = column_sum(0)
-    for k in (2, 3, 1):
-        take(rz.at[k], RZ + k)
-        total = total + rz[k].astype(jnp.float32)
+    take(rz, RZ)
+    total = total + rz[...].astype(jnp.float32)
     ids = g * 16 + lax.broadcasted_iota(jnp.int32, total.shape, 0)
     fin[...] = jnp.where(ids < length, own_rows[...] + total, 0.0).astype(jnp.bfloat16)
     push(fin, fin_in, BACK, BACK, sibling)
@@ -341,12 +369,14 @@
             pltpu.VMEM(wide_table.shape, f32),
             pltpu.VMEM(tall_table.shape, f32),
             pltpu.VMEM((span, head_size), bf16),
-            pltpu.VMEM((2, 8, 32, 128), bf16),
+            pltpu.VMEM((2, 4, 2, 32, 128), bf16),
             pltpu.VMEM((span // 2, 2 * head_size), bf16),
-            pltpu.VMEM((4, rows, width), f32),
+            pltpu.VMEM((8, rows, width), f32),
             pltpu.VMEM((8, rows, width), bf16),
-            pltpu.VMEM((4, rows, width), bf16),
-            pltpu.VMEM((4, rows, width), bf16),
+            pltpu.VMEM((2, rows, width), bf16),
+            pltpu.VMEM((2, rows, width), bf16),
+            pltpu.VMEM((2, rows, width), bf16),
+            pltpu.VMEM((rows, width), bf16),
             pltpu.VMEM((rows, width), bf16),
             pltpu.VMEM((rows, width), bf16),
             pltpu.SemaphoreType.DMA((COUNT,)),

time: 39.1 us -> 43.4 us (1.11)
  Pallas kernels: 37.4 us -> 41.7 us
    pallas_call x1, Pallas kernels: 37.4 us -> 41.7 us  [fused(): pl.pallas_call(span_kernel, out_shape=jax.ShapeDtypeStruct(hidden_in.shap...]
where the time goes in v5:
time: 43.4 us; the launch traced here: 43.3 us
  Pallas kernels  41.7 us (96%)
  local copies, waits for them, and re-layouts  1.57 us (4%)
    pallas_call x1, Pallas kernels, fused(): pl.pallas_call(span_kernel, out_shape=jax.ShapeDtypeStruct(hidden_in.shap...  41.7 us
    unnamed x1, local copies, waits for them, and re-layouts  1.57 us

profile of v5, /device:TPU:0, one launch (start us, length us, event | category | flops | bytes accessed | tf_op | source)
XLA Modules:
  0.0 43.3 jit_solution(13469797266934991035)
XLA Ops:
  0.0 41.7 %shard_map.91 = bf16[2,16,2048]{2,1,0:T(8,128)(2,1)} custom-call(s32[4]{0:T(128)} %lens.1, bf16[2,16,2048]{2,1,0:T(8,128)(2,1)} %hidden.1, bf16[2048]{0:T(1024)(128)(2,1)} %gain.1, bf16[2048,128]{1,0:T(8,128)(2,1)} %wq.1, bf16[16,2048]{1,0:T(8,128)(2,1)} %bitcast.2, bf16[16,2048]{1,0:T(8,128)(2,1)} %bitcast.3, bf16[128,2048]{1,0:T(8,128)(2,1)} %wo.1, ...), custom_call_target="tpu_custom_call" | custom-call | flops 268435456 | bytes 1048576 | tf_op jit(solution)/shard_map/pallas_call | solution.py:355
  41.7 1.6 %copy.11 = bf16[2,16,2048]{2,1,0:T(8,128)(2,1)} copy(bf16[2,16,2048]{2,1,0:T(8,128)(2,1)} %shard_map.91) | data formatting | bytes 262144

commit v6 on v5

--- a/solution.py
+++ b/solution.py
@@ -198,10 +198,6 @@
     def out_half(at):
         return out_rows(at, 64, d * 64)
 
-    push(wq.at[half_q], query_half(plane), WEIGHT, WEIGHT, partner)
-    push(wk.at[:, half_q], key_half(plane, 0), WEIGHT + 1, WEIGHT + 1, partner)
-    push(wv.at[:, half_q], key_half(plane, 1), WEIGHT + 2, WEIGHT + 2, partner)
-
     for load in early:
         load.wait()
     busy = jnp.where(lens[0] > 0, 0, 1)
@@ -225,6 +221,9 @@
 
     push(block(0, 0), block(0, 0), GZ, GZ, far)
     spread(0)
+    push(wq.at[half_q], query_half(plane), WEIGHT, WEIGHT, partner)
+    push(wk.at[:, half_q], key_half(plane, 0), WEIGHT + 1, WEIGHT + 1, partner)
+    push(wv.at[:, half_q], key_half(plane, 1), WEIGHT + 2, WEIGHT + 2, partner)
     push(wo.at[pl.ds(d * 64, 64)], out_half(plane), WEIGHT + 3, WEIGHT + 3, partner)
     take(block(0, 1), GZ)
     spread(1)

time: 43.4 us -> 41.9 us (0.965)
  Pallas kernels: 41.7 us -> 40.2 us
    pallas_call x1, Pallas kernels: 41.7 us -> 40.2 us  [fused(): pl.pallas_call(span_kernel, out_shape=jax.ShapeDtypeStruct(hidden_in.shap...]
where the time goes in v6:
time: 41.9 us; the launch traced here: 41.7 us
  Pallas kernels  40.2 us (96%)
  local copies, waits for them, and re-layouts  1.57 us (4%)
    pallas_call x1, Pallas kernels, fused(): pl.pallas_call(span_kernel, out_shape=jax.ShapeDtypeStruct(hidden_in.shap...  40.2 us
    unnamed x1, local copies, waits for them, and re-layouts  1.57 us

profile of v6, /device:TPU:0, one launch (start us, length us, event | category | flops | bytes accessed | tf_op | source)
XLA Modules:
  0.0 41.7 jit_solution(2638659162768754018)
XLA Ops:
  0.0 40.2 %shard_map.91 = bf16[2,16,2048]{2,1,0:T(8,128)(2,1)} custom-call(s32[4]{0:T(128)} %lens.1, bf16[2,16,2048]{2,1,0:T(8,128)(2,1)} %hidden.1, bf16[2048]{0:T(1024)(128)(2,1)} %gain.1, bf16[2048,128]{1,0:T(8,128)(2,1)} %wq.1, bf16[16,2048]{1,0:T(8,128)(2,1)} %bitcast.2, bf16[16,2048]{1,0:T(8,128)(2,1)} %bitcast.3, bf16[128,2048]{1,0:T(8,128)(2,1)} %wo.1, ...), custom_call_target="tpu_custom_call" | custom-call | flops 268435456 | bytes 1048576 | tf_op jit(solution)/shard_map/pallas_call | solution.py:354
  40.2 1.6 %copy.11 = bf16[2,16,2048]{2,1,0:T(8,128)(2,1)} copy(bf16[2,16,2048]{2,1,0:T(8,128)(2,1)} %shard_map.91) | data formatting | bytes 262144
